TPU v7x, 256 devices: a whole 4x4x8 slice. The times are simulated.
256 devices in a mesh: dp: 32 (over y, x, core), seq: 8 (over z).
Axes of the slice: x: 4, y: 4, z: 8, core: 2. Of those that a mesh axis runs over, the one named last changes fastest.
Arguments:
- t5_attn: bfloat16 [32, 128, 2048], P('dp', None, 'seq'), may hold values from -6 to 6
- t5_out_w: bfloat16 [2048, 4096], P('seq'), may hold values from -0.125 to 0.125
- t5_resid: bfloat16 [32, 128, 4096], P('dp', None, 'seq'), may hold values from -6 to 6
- text_dest: int32 [32, 128, 1], P('dp'), may hold values from 0 to 31; in each aligned block of 128 rows (0 to 127, 128 to 255, ..., all dimensions but the last counted through in order) at most 8 rows name the same one
- text_sample: int32 [32, 128], P('dp'), may hold values from 0 to 3
- kv_weight: bfloat16 [4096, 2, 2048], P(None, None, 'seq'), may hold values from -0.09375 to 0.09375
- img_query: bfloat16 [32, 2048, 2048], P('dp', 'seq'), may hold values from -32 to 32
- img_key: bfloat16 [32, 2048, 2048], P('dp', 'seq'), may hold values from -32 to 32
- img_value: bfloat16 [32, 2048, 2048], P('dp', 'seq'), may hold values from -6 to 6
- img_sample: int32 [32, 2048], P('dp'), may hold values from 0 to 3, never falling along the last dimension, each value on 1 to 1024 neighbouring positions
- proj_weight: bfloat16 [2048, 1536], P(('dp', 'seq')), may hold values from -0.125 to 0.125
- gate: float32 [32, 4, 1536], P('dp'), may hold values from -4 to 4
Outputs:
- block_out: bfloat16 [32, 2048, 1536], P('dp', 'seq')
Inputs may be any that keep to these rules, and one draw needn't show every extreme that they name: `text_dest`: among the 128 text rows of one group at most 8 name the same destination group, and exactly 8 do so for some pair in every draw; every group is named by some row. `img_sample`: along a group's 2048 tokens the sample number never falls; every sample has 1 to 1024 tokens and one has exactly 1024.
All inputs are finite; a program needn't handle non-finite values.
Results may differ from a plain program's by a relative error of at most 0.018.
Values may be sent and summed in bfloat16 or wider, within the bound.
No kernel may reach another device: no remote copies, remote signals or barrier semaphores. Data moves between devices by JAX's collectives and lax.ppermute only.
A program may use at most 128 MiB of HBM per device.

v0:
```python
import math

import jax
import jax.numpy as jnp
from jax import lax
from jax.sharding import PartitionSpec as P

HEAD_DIM = 128


def text_projection(text_rows, kv_weight):
    features = kv_weight.shape[0]
    local_width = kv_weight.shape[2]
    row_count = text_rows.shape[0]
    projected_kv = jnp.dot(
        text_rows, kv_weight.reshape(features, 2 * local_width), preferred_element_type=jnp.float32
    )
    key_part = projected_kv[:, :local_width].reshape(row_count, local_width // HEAD_DIM, HEAD_DIM)
    key_part = key_part * lax.rsqrt(jnp.mean(key_part * key_part, axis=-1, keepdims=True) + 1e-06)
    text_keys = key_part.reshape(row_count, local_width).astype(jnp.bfloat16)
    text_values = projected_kv[:, local_width:].astype(jnp.bfloat16)
    return (text_keys, text_values)


def on_device(
    t5_attn,
    t5_out_w,
    t5_resid,
    text_dest,
    text_sample,
    kv_weight,
    img_query,
    img_key,
    img_value,
    img_sample,
    proj_weight,
    gate,
):
    groups = lax.axis_size("dp")
    lane = lax.axis_index("seq")
    text_count = t5_attn.shape[1]
    capacity = 2 * text_count // groups
    feat_block = t5_resid.shape[2]
    partial_value = jnp.dot(t5_attn[0], t5_out_w, preferred_element_type=jnp.float32)
    own_cols = lax.dynamic_slice_in_dim(partial_value, lane * feat_block, feat_block, 1)
    partial_value = lax.dynamic_update_slice_in_dim(
        partial_value, own_cols + t5_resid[0].astype(jnp.float32), lane * feat_block, 1
    )
    t5_term = partial_value.astype(jnp.bfloat16)
    t5_layer = lax.psum(t5_term, "seq").astype(jnp.float32).astype(jnp.bfloat16)
    target = text_dest[0, :, 0]
    one_hot = (target[:, None] == jnp.arange(groups, dtype=jnp.int32)[None, :]).astype(jnp.int32)
    rank_of = jnp.sum((jnp.cumsum(one_hot, axis=0) - one_hot) * one_hot, axis=1)
    slot_of = target * capacity + rank_of
    row_of = (
        jnp.full((groups * capacity,), -1, jnp.int32)
        .at[slot_of]
        .set(jnp.arange(text_count, dtype=jnp.int32))
    )
    filled = row_of >= 0
    safe_row = jnp.maximum(row_of, 0)
    slot_sample = jnp.where(filled, text_sample[0][safe_row], -1)
    zero_value = jnp.zeros((), jnp.bfloat16)
    send_rows = jnp.where(filled[:, None], t5_layer[safe_row], zero_value)
    arrived, sample_text = (
        lax.all_to_all(send_rows, "dp", split_axis=0, concat_axis=0, tiled=True),
        lax.all_to_all(slot_sample, "dp", split_axis=0, concat_axis=0, tiled=True),
    )
    text_keys, text_values = text_projection(arrived, kv_weight)
    queries, image_keys, image_values = (
        lax.all_to_all(img_query[0], "seq", split_axis=1, concat_axis=0, tiled=True),
        lax.all_to_all(img_key[0], "seq", split_axis=1, concat_axis=0, tiled=True),
        lax.all_to_all(img_value[0], "seq", split_axis=1, concat_axis=0, tiled=True),
    )
    group_rows = queries.shape[0]
    heads_dev = queries.shape[1] // HEAD_DIM
    all_keys = jnp.concatenate([image_keys, text_keys], axis=0).reshape(-1, heads_dev, HEAD_DIM)
    all_values = jnp.concatenate([image_values, text_values], axis=0).reshape(
        -1, heads_dev, HEAD_DIM
    )
    query_sample = img_sample[0]
    key_sample = jnp.concatenate([query_sample, sample_text])
    score_scale = 1.0 / math.sqrt(HEAD_DIM)
    block_rows = math.gcd(group_rows, 512)

    def attend(block_inputs):
        query_rows, row_sample = block_inputs
        scores = (
            jnp.einsum("qhd,khd->hqk", query_rows, all_keys, preferred_element_type=jnp.float32)
            * score_scale
        )
        allowed = row_sample[:, None] == key_sample[None, :]
        scores = jnp.where(allowed[None], scores, -jnp.inf)
        largest = jnp.max(scores, axis=-1, keepdims=True)
        exponent = jnp.exp(scores - largest)
        weights = (exponent / jnp.sum(exponent, axis=-1, keepdims=True)).astype(jnp.bfloat16)
        attended = jnp.einsum(
            "hqk,khd->qhd", weights, all_values, preferred_element_type=jnp.float32
        )
        return attended.astype(jnp.bfloat16).reshape(query_rows.shape[0], -1)

    attended = lax.map(
        attend,
        (
            queries.reshape(group_rows // block_rows, block_rows, heads_dev, HEAD_DIM),
            query_sample.reshape(group_rows // block_rows, block_rows),
        ),
    )
    attended = attended.reshape(group_rows, -1)
    returned = lax.all_to_all(attended, "seq", split_axis=0, concat_axis=1, tiled=True)
    token_count = returned.shape[0]
    projected = jnp.dot(
        returned,
        lax.all_gather(proj_weight, ("dp", "seq"), axis=0, tiled=True),
        preferred_element_type=jnp.float32,
    )
    own_sample = lax.dynamic_slice_in_dim(img_sample[0], lane * token_count, token_count)
    sample_hot = (
        own_sample[:, None] == jnp.arange(gate.shape[1], dtype=jnp.int32)[None, :]
    ).astype(jnp.float32)
    gate_rows = jnp.sum(sample_hot[:, :, None] * gate[0][None, :, :], axis=1)
    return (gate_rows * projected).astype(jnp.bfloat16)[None]


def solution(mesh):
    placed = (
        P("dp", None, "seq"),
        P("seq", None),
        P("dp", None, "seq"),
        P("dp", None, None),
        P("dp", None),
        P(None, None, "seq"),
        P("dp", "seq", None),
        P("dp", "seq", None),
        P("dp", "seq", None),
        P("dp", None),
        P(("dp", "seq"), None),
        P("dp", None, None),
    )
    return jax.shard_map(
        on_device, mesh=mesh, in_specs=placed, out_specs=P("dp", "seq", None), check_vma=False
    )
```

profile of v0, /device:TPU:20, one launch (start us, length us, event | category | flops | bytes accessed | tf_op | source)
XLA Modules:
  0.0 324.5 jit_solution(18062396501500716525)
XLA Ops:
  13.6 7.4 %all-to-all-start = ((s32[32,8,1]{1,2,0:T(1,128)}), s32[32,8,1]{1,2,0:T(1,128)S(1)}, u32[]{:S(2)}, u32[]{:S(2)}) async-start(s32[32,8,1]{1,2,0:T(1,128)} %bitcast.12), calls=%async_computation | async-start | bytes 32768 | tf_op jit(solution)/shard_map/all_to_all | solution.py:67
  24.3 8.5 %all-to-all-start.2 = ((bf16[256,8,256]{0,2,1:T(8,128)(2,1)}), bf16[256,8,256]{0,2,1:T(8,128)(2,1)S(1)}, u32[]{:S(2)}, u32[]{:S(2)}) async-start(bf16[256,8,256]{0,2,1:T(8,128)(2,1)} %bitcast.98), calls=%async_computation.2 | async-start | bytes 2097152 | tf_op jit(solution)/shard_map/all_to_all | solution.py:72
  35.1 26.4 %all-to-all-done.2 = bf16[256,8,256]{0,2,1:T(8,128)(2,1)S(1)} async-done(((bf16[256,8,256]{0,2,1:T(8,128)(2,1)}), bf16[256,8,256]{0,2,1:T(8,128)(2,1)S(1)}, u32[]{:S(2)}, u32[]{:S(2)}) %all-to-all-start.2) | async-done | bytes 1048608 | tf_op jit(solution)/shard_map/all_to_all | solution.py:72
  61.6 4.2 %all-to-all-start.4 = ((bf16[256,8,256]{0,2,1:T(8,128)(2,1)}), bf16[256,8,256]{0,2,1:T(8,128)(2,1)}, u32[]{:S(2)}, u32[]{:S(2)}) async-start(bf16[256,8,256]{0,2,1:T(8,128)(2,1)} %bitcast.96), calls=%async_computation.4 | async-start | bytes 2097152 | tf_op jit(solution)/shard_map/all_to_all | solution.py:73
  70.8 26.8 %all-to-all-done.4 = bf16[256,8,256]{0,2,1:T(8,128)(2,1)} async-done(((bf16[256,8,256]{0,2,1:T(8,128)(2,1)}), bf16[256,8,256]{0,2,1:T(8,128)(2,1)}, u32[]{:S(2)}, u32[]{:S(2)}) %all-to-all-start.4) | async-done | bytes 1048608 | tf_op jit(solution)/shard_map/all_to_all | solution.py:73
  97.5 4.2 %all-to-all-start.1 = ((bf16[256,8,256]{2,0,1:T(8,128)(2,1)}), bf16[256,8,256]{2,0,1:T(8,128)(2,1)}, u32[]{:S(2)}, u32[]{:S(2)}) async-start(bf16[256,8,256]{2,0,1:T(8,128)(2,1)} %copy.74), calls=%async_computation.1 | async-start | bytes 2097152 | tf_op jit(solution)/shard_map/all_to_all | solution.py:71
  101.9 56.3 %all-reduce.2.cloned.1.call-done = bf16[128,4096]{1,0:T(8,128)(2,1)} async-done(((bf16[128,4096]{1,0:T(8,128)(2,1)}), bf16[128,4096]{1,0:T(8,128)(2,1)}) %all-reduce.2.cloned.1.call-update) | async-done | bytes 1048592 | tf_op jit(solution)/shard_map/psum | solution.py:50
  158.2 6.6 %gather_fusion.1 = bf16[256,4096]{1,0:T(8,128)(2,1)} fusion(bf16[128,4096]{1,0:T(8,128)(2,1)} %all-reduce.2.cloned.1.call-done, s32[1024]{0:T(1024)S(1)} %pad_clamp_fusion), kind=kCustom, calls=%fused_computation.1 | custom fusion | bytes 4195328 | tf_op jit(solution)/shard_map/gather | solution.py:64
  167.9 7.4 %all-to-all-start.3 = ((bf16[32,8,4096]{2,1,0:T(8,128)(2,1)}), bf16[32,8,4096]{2,1,0:T(8,128)(2,1)}, u32[]{:S(2)}, u32[]{:S(2)}) async-start(bf16[32,8,4096]{2,1,0:T(8,128)(2,1)} %bitcast_select_fusion), calls=%async_computation.3 | async-start | bytes 4194304 | tf_op jit(solution)/shard_map/all_to_all | solution.py:66
  175.9 5.0 %copy.93 = bf16[512,8,2,256]{3,1,2,0:T(8,128)(2,1)} copy(bf16[512,8,2,256]{3,2,1,0:T(2,128)(2,1)} %bitcast.93) | data formatting | bytes 8388608
  192.7 7.3 %all-to-all-done.3 = bf16[32,8,4096]{2,1,0:T(8,128)(2,1)} async-done(((bf16[32,8,4096]{2,1,0:T(8,128)(2,1)}), bf16[32,8,4096]{2,1,0:T(8,128)(2,1)}, u32[]{:S(2)}, u32[]{:S(2)}) %all-to-all-start.3) | async-done | bytes 2097184 | tf_op jit(solution)/shard_map/all_to_all | solution.py:66
  200.0 4.1 %fusion.18 = f32[256,512]{1,0:T(8,128)S(1)} fusion(bf16[4096,512]{1,0:T(8,128)(2,1)} %bitcast.94, bf16[32,8,4096]{2,1,0:T(8,128)(2,1)} %all-to-all-done.3), kind=kOutput, calls=%fused_computation.28 | convolution fusion | flops 1073741824 | bytes 6815744 | tf_op jit(solution)/shard_map/dot_general | solution.py:15
  210.4 61.6 %while.10 = (s32[]{:T(128)}, bf16[4,512,256]{2,1,0:T(8,128)(2,1)}, s32[4,512]{1,0:T(4,128)}, s32[2304]{0:T(1024)S(1)}, bf16[4,512,2,128]{3,2,1,0:T(2,128)(2,1)},...) while((s32[]{:T(128)}, bf16[4,512,256]{2,1,0:T(8,128)(2,1)}, ...), condition=%wide.region_9.10_spmd, body=%wide.region_6.9_spmd.sunk | while | flops 1834489344 | bytes 9461341 | solution.py:102
  212.9 4.7 %fusion.45 = f32[2,512]{1,0:T(2,128)S(1)} fusion(pred[512,2304]{1,0:T(8,128)(4,1)S(1)} %broadcast_compare_fusion.4, bf16[2304,2,128]{2,0,1:T(8,128)(2,1)} %get-tuple-element.165, bf16[1,512,2,128]{3,2,1,0:T(2,128)(2,1)S(1)} %constant_dynamic-slice_fusion.6), kind=kOutput, calls=%fused_computation.58.clone.1 | convolution fusion | flops 613419264 | bytes 2625536 | tf_op jit(solution)/shard_map/while/body/eval_jaxpr/sub | solution.py:95
  217.6 6.3 %fusion.46 = bf16[2,512,128]{1,2,0:T(8,128)(2,1)} fusion(bf16[2304,2,128]{0,2,1:T(8,128)(2,1)} %get-tuple-element.166, f32[2,512]{1,0:T(2,128)S(1)} %fusion.45, pred[512,2304]{1,0:T(8,128)(4,1)S(1)} %broadcast_compare_fusion.4, bf16[2304,2,128]{2,0,1:T(8,128)(2,1)} %get-tuple-element.165, bf16[1,512,2,128]{3,2,1,0:T(2,128)(2,1)S(1)} %constant_dynamic-slice_fusion.6), kind=kOutput, calls=%fused_computation.14.clone.1 | convolution fusion | flops 1219890432 | bytes 4067328 | tf_op jit(solution)/shard_map/while/body/eval_jaxpr/hqk,khd->qhd/dot_general | solution.py:97
  228.3 4.7 %fusion.45 = f32[2,512]{1,0:T(2,128)S(1)} fusion(pred[512,2304]{1,0:T(8,128)(4,1)S(1)} %broadcast_compare_fusion.4, bf16[2304,2,128]{2,0,1:T(8,128)(2,1)} %get-tuple-element.165, bf16[1,512,2,128]{3,2,1,0:T(2,128)(2,1)S(1)} %constant_dynamic-slice_fusion.6), kind=kOutput, calls=%fused_computation.58.clone.1 | convolution fusion | flops 613419264 | bytes 2625536 | tf_op jit(solution)/shard_map/while/body/eval_jaxpr/sub | solution.py:95
  233.0 6.3 %fusion.46 = bf16[2,512,128]{1,2,0:T(8,128)(2,1)} fusion(bf16[2304,2,128]{0,2,1:T(8,128)(2,1)} %get-tuple-element.166, f32[2,512]{1,0:T(2,128)S(1)} %fusion.45, pred[512,2304]{1,0:T(8,128)(4,1)S(1)} %broadcast_compare_fusion.4, bf16[2304,2,128]{2,0,1:T(8,128)(2,1)} %get-tuple-element.165, bf16[1,512,2,128]{3,2,1,0:T(2,128)(2,1)S(1)} %constant_dynamic-slice_fusion.6), kind=kOutput, calls=%fused_computation.14.clone.1 | convolution fusion | flops 1219890432 | bytes 4067328 | tf_op jit(solution)/shard_map/while/body/eval_jaxpr/hqk,khd->qhd/dot_general | solution.py:97
  243.7 4.7 %fusion.45 = f32[2,512]{1,0:T(2,128)S(1)} fusion(pred[512,2304]{1,0:T(8,128)(4,1)S(1)} %broadcast_compare_fusion.4, bf16[2304,2,128]{2,0,1:T(8,128)(2,1)} %get-tuple-element.165, bf16[1,512,2,128]{3,2,1,0:T(2,128)(2,1)S(1)} %constant_dynamic-slice_fusion.6), kind=kOutput, calls=%fused_computation.58.clone.1 | convolution fusion | flops 613419264 | bytes 2625536 | tf_op jit(solution)/shard_map/while/body/eval_jaxpr/sub | solution.py:95
  248.4 6.3 %fusion.46 = bf16[2,512,128]{1,2,0:T(8,128)(2,1)} fusion(bf16[2304,2,128]{0,2,1:T(8,128)(2,1)} %get-tuple-element.166, f32[2,512]{1,0:T(2,128)S(1)} %fusion.45, pred[512,2304]{1,0:T(8,128)(4,1)S(1)} %broadcast_compare_fusion.4, bf16[2304,2,128]{2,0,1:T(8,128)(2,1)} %get-tuple-element.165, bf16[1,512,2,128]{3,2,1,0:T(2,128)(2,1)S(1)} %constant_dynamic-slice_fusion.6), kind=kOutput, calls=%fused_computation.14.clone.1 | convolution fusion | flops 1219890432 | bytes 4067328 | tf_op jit(solution)/shard_map/while/body/eval_jaxpr/hqk,khd->qhd/dot_general | solution.py:97
  259.2 4.7 %fusion.45 = f32[2,512]{1,0:T(2,128)S(1)} fusion(pred[512,2304]{1,0:T(8,128)(4,1)S(1)} %broadcast_compare_fusion.4, bf16[2304,2,128]{2,0,1:T(8,128)(2,1)} %get-tuple-element.165, bf16[1,512,2,128]{3,2,1,0:T(2,128)(2,1)S(1)} %constant_dynamic-slice_fusion.6), kind=kOutput, calls=%fused_computation.58.clone.1 | convolution fusion | flops 613419264 | bytes 2625536 | tf_op jit(solution)/shard_map/while/body/eval_jaxpr/sub | solution.py:95
  263.8 6.3 %fusion.46 = bf16[2,512,128]{1,2,0:T(8,128)(2,1)} fusion(bf16[2304,2,128]{0,2,1:T(8,128)(2,1)} %get-tuple-element.166, f32[2,512]{1,0:T(2,128)S(1)} %fusion.45, pred[512,2304]{1,0:T(8,128)(4,1)S(1)} %broadcast_compare_fusion.4, bf16[2304,2,128]{2,0,1:T(8,128)(2,1)} %get-tuple-element.165, bf16[1,512,2,128]{3,2,1,0:T(2,128)(2,1)S(1)} %constant_dynamic-slice_fusion.6), kind=kOutput, calls=%fused_computation.14.clone.1 | convolution fusion | flops 1219890432 | bytes 4067328 | tf_op jit(solution)/shard_map/while/body/eval_jaxpr/hqk,khd->qhd/dot_general | solution.py:97
  272.0 4.3 %all-to-all-start.5 = ((bf16[8,256,256]{2,1,0:T(8,128)(2,1)}), bf16[8,256,256]{2,1,0:T(8,128)(2,1)S(1)}, u32[]{:S(2)}, u32[]{:S(2)}) async-start(bf16[8,256,256]{2,1,0:T(8,128)(2,1)} %bitcast.101), calls=%async_computation.5 | async-start | bytes 2097152 | tf_op jit(solution)/shard_map/all_to_all | solution.py:110
  278.6 29.9 %all-to-all-done.5 = bf16[8,256,256]{2,1,0:T(8,128)(2,1)S(1)} async-done(((bf16[8,256,256]{2,1,0:T(8,128)(2,1)}), bf16[8,256,256]{2,1,0:T(8,128)(2,1)S(1)}, u32[]{:S(2)}, u32[]{:S(2)}) %all-to-all-start.5) | async-done | bytes 1048608 | tf_op jit(solution)/shard_map/all_to_all | solution.py:110
  311.1 5.9 %fusion.17 = bf16[1,256,1536]{2,1,0:T(8,128)(2,1)} fusion(f32[256,1536]{1,0:T(8,128)} %multiply_reduce_fusion, bf16[256,2048]{0,1:T(8,128)(2,1)S(1)} %bitcast.91, bf16[2048,1536]{1,0:T(8,128)(2,1)} %all-gather.2.cloned.1.call-done), kind=kOutput, calls=%fused_computation.27 | convolution fusion | flops 1611399168 | bytes 9699328 | tf_op jit(solution)/shard_map/dot_general | solution.py:112
  (89 shorter events, 60.9 us)
Async XLA Ops:
  7.4 58.5 %copy-start = (bf16[256,4096]{1,0:T(8,128)(2,1)S(1)}, bf16[256,4096]{1,0:T(8,128)(2,1)}, u32[]{:S(2)}) copy-start(bf16[256,4096]{1,0:T(8,128)(2,1)} %param.15) | copy-start | bytes 6291460
  7.4 13.6 %copy-start.2 = (bf16[1,256,2048]{2,1,0:T(8,128)(2,1)S(1)}, bf16[1,256,2048]{2,1,0:T(8,128)(2,1)}, u32[]{:S(2)}) copy-start(bf16[1,256,2048]{2,1,0:T(8,128)(2,1)} %param.21) | copy-start | bytes 3145732
  13.6 10.8 %all-to-all-start = ((s32[32,8,1]{1,2,0:T(1,128)}), s32[32,8,1]{1,2,0:T(1,128)S(1)}, u32[]{:S(2)}, u32[]{:S(2)}) async-start(s32[32,8,1]{1,2,0:T(1,128)} %bitcast.12), calls=%async_computation | async-start | bytes 32768 | tf_op jit(solution)/shard_map/all_to_all | solution.py:67
  24.3 37.2 %all-to-all-start.2 = ((bf16[256,8,256]{0,2,1:T(8,128)(2,1)}), bf16[256,8,256]{0,2,1:T(8,128)(2,1)S(1)}, u32[]{:S(2)}, u32[]{:S(2)}) async-start(bf16[256,8,256]{0,2,1:T(8,128)(2,1)} %bitcast.98), calls=%async_computation.2 | async-start | bytes 2097152 | tf_op jit(solution)/shard_map/all_to_all | solution.py:72
  32.8 33.1 %copy-start.4 = (bf16[1,128,256]{2,1,0:T(8,128)(2,1)S(1)}, bf16[1,128,256]{2,1,0:T(8,128)(2,1)}, u32[]{:S(2)}) copy-start(bf16[1,128,256]{2,1,0:T(8,128)(2,1)} %param.14) | copy-start | bytes 196612
  61.6 36.0 %all-to-all-start.4 = ((bf16[256,8,256]{0,2,1:T(8,128)(2,1)}), bf16[256,8,256]{0,2,1:T(8,128)(2,1)}, u32[]{:S(2)}, u32[]{:S(2)}) async-start(bf16[256,8,256]{0,2,1:T(8,128)(2,1)} %bitcast.96), calls=%async_computation.4 | async-start | bytes 2097152 | tf_op jit(solution)/shard_map/all_to_all | solution.py:73
  65.8 92.4 %all-reduce.2.cloned.1.call-start = ((), (), s32[]{:S(2)}) async-start(), calls=%async_computation.6 | async-start | bytes 2097152 | tf_op jit(solution)/shard_map/psum | solution.py:50
  65.9 0.9 copy-start.3
  97.5 70.4 %all-to-all-start.1 = ((bf16[256,8,256]{2,0,1:T(8,128)(2,1)}), bf16[256,8,256]{2,0,1:T(8,128)(2,1)}, u32[]{:S(2)}, u32[]{:S(2)}) async-start(bf16[256,8,256]{2,0,1:T(8,128)(2,1)} %copy.74), calls=%async_computation.1 | async-start | bytes 2097152 | tf_op jit(solution)/shard_map/all_to_all | solution.py:71
  167.9 32.1 %all-to-all-start.3 = ((bf16[32,8,4096]{2,1,0:T(8,128)(2,1)}), bf16[32,8,4096]{2,1,0:T(8,128)(2,1)}, u32[]{:S(2)}, u32[]{:S(2)}) async-start(bf16[32,8,4096]{2,1,0:T(8,128)(2,1)} %bitcast_select_fusion), calls=%async_computation.3 | async-start | bytes 4194304 | tf_op jit(solution)/shard_map/all_to_all | solution.py:66
  175.3 135.7 %all-gather.2.cloned.1.call-start = ((), (), s32[]{:S(2)}) async-start(), calls=%async_computation.7 | async-start | bytes 6316032 | tf_op jit(solution)/shard_map/all_gather | solution.py:114
  175.9 5.5 %copy-start.5 = (s32[1,2048]{1,0:T(1,128)S(1)}, s32[1,2048]{1,0:T(1,128)}, u32[]{:S(2)}) copy-start(s32[1,2048]{1,0:T(1,128)} %param.23) | copy-start | bytes 24580
  272.0 5.0 %copy-start.6 = (f32[1,4,1536]{2,1,0:T(4,128)S(1)}, f32[1,4,1536]{2,1,0:T(4,128)}, u32[]{:S(2)}) copy-start(f32[1,4,1536]{2,1,0:T(4,128)} %param.25) | copy-start | bytes 73732
  272.0 36.5 %all-to-all-start.5 = ((bf16[8,256,256]{2,1,0:T(8,128)(2,1)}), bf16[8,256,256]{2,1,0:T(8,128)(2,1)S(1)}, u32[]{:S(2)}, u32[]{:S(2)}) async-start(bf16[8,256,256]{2,1,0:T(8,128)(2,1)} %bitcast.101), calls=%async_computation.5 | async-start | bytes 2097152 | tf_op jit(solution)/shard_map/all_to_all | solution.py:110
  308.5 1.1 copy-start.1
Sparse Core Ops, SparseCore 0:
  69.0 89.1 all-reduce.1
Sparse Core Ops, SparseCore 1:
  179.7 126.1 all-gather.1
where the time goes:
time: 331 us; the launch traced here: 324 us
  waiting for transfers between devices  149 us (45%)
  matrix products  54.4 us (16%)
  local copies, waits for them, and re-layouts  52.4 us (16%)
  starting transfers between devices  36.1 us (11%)
  other arithmetic  16.9 us (5%)
  between operations  15.1 us (5%)
    psum x1, waiting for transfers between devices, on_device(): t5_layer = lax.psum(t5_term, 'seq').astype(jnp.float32).astype(jnp.bfloat16)  56.3 us
    all_to_all x1, waiting for transfers between devices, on_device(): lax.all_to_all(attended, 'seq', split_axis=0, concat_axis=1, tiled=True)  29.9 us
    all_to_all x1, waiting for transfers between devices, on_device(): lax.all_to_all(img_value[0], 'seq', split_axis=1, concat_axis=0, tiled=True)  26.8 us
    all_to_all x1, waiting for transfers between devices, on_device(): lax.all_to_all(img_key[0], 'seq', split_axis=1, concat_axis=0, tiled=True)  26.4 us
    dot_general x4, matrix products, attend(): jnp.einsum('hqk,khd->qhd', weights, all_values, preferred_element_type=jn...  25.3 us
    sub x4, matrix products, attend(): exponent = jnp.exp(scores - largest)  18.7 us
    unnamed x19, local copies, waits for them, and re-layouts  12.2 us
    all_to_all x1, starting transfers between devices, on_device(): lax.all_to_all(img_key[0], 'seq', split_axis=1, concat_axis=0, tiled=True)  8.47 us
  transfers between devices with their start and end apart: 8, of which 6 were waited for; matrix products, arithmetic and copies ran while one was open for 34% of the time, Pallas kernels for 0%

commit v1 on v0

v1 whole, which is shorter than its diff:
```python
import functools
import math

import jax
import jax.numpy as jnp
from jax import lax
from jax.experimental import pallas as pl
from jax.experimental.pallas import tpu as pltpu
from jax.sharding import PartitionSpec as P

HEAD_DIM = 128
PENALTY = 524288.0
CHUNK = 512
BF16 = jnp.bfloat16
F32 = jnp.float32
VMEM = pl.BlockSpec(memory_space=pltpu.VMEM)
SMEM = pl.BlockSpec(memory_space=pltpu.SMEM)
ANY = pl.BlockSpec(memory_space=pl.ANY)
PARAMS = pltpu.CompilerParams(vmem_limit_bytes=48 * 1024 * 1024)


def pack_kernel(lanes, lane_ref, q_ref, k_ref, v_ref, *refs):
    kv_out, q_out, sems = refs[:lanes], refs[lanes : 2 * lanes], refs[2 * lanes]
    width = q_ref.shape[1] // lanes
    copies = []
    for step in range(lanes):
        shift = (step + 4) % lanes
        owner = lax.rem(lane_ref[0] + shift, lanes)
        cols = pl.ds(pl.multiple_of(owner * width, width), width)
        copies.append(pltpu.make_async_copy(k_ref.at[:, cols], kv_out[shift].at[0], sems.at[3 * shift]))
        copies.append(pltpu.make_async_copy(v_ref.at[:, cols], kv_out[shift].at[1], sems.at[3 * shift + 1]))
        copies.append(pltpu.make_async_copy(q_ref.at[:, cols], q_out[shift], sems.at[3 * shift + 2]))
    for copy in copies:
        copy.start()
    for copy in copies:
        copy.wait()


def pack(lanes, lane, query, key, value):
    rows, features = query.shape
    width = features // lanes
    return pl.pallas_call(
        functools.partial(pack_kernel, lanes),
        out_shape=[jax.ShapeDtypeStruct((2, rows, width), BF16)] * lanes
        + [jax.ShapeDtypeStruct((rows, width), BF16)] * lanes,
        in_specs=[SMEM, ANY, ANY, ANY],
        out_specs=[ANY] * (2 * lanes),
        scratch_shapes=[pltpu.SemaphoreType.DMA((3 * lanes,))],
        name="pack",
    )(lane, query, key, value)


def text_kernel(steps, t5_ref, map_ref, kvw_ref, slot_ref, sample_ref, out_ref, total):
    step = pl.program_id(0)
    inner = map_ref.shape[0]

    @pl.when(step == 0)
    def _():
        total[...] = jnp.zeros_like(total)

    rows = t5_ref[0]
    total[...] += jnp.dot(rows[:, :inner], map_ref[...], preferred_element_type=F32) + jnp.dot(
        rows[:, inner:], kvw_ref[...], preferred_element_type=F32
    )

    @pl.when(step == steps - 1)
    def _():
        width = total.shape[1] // 2
        parts = []
        for head in range(width // HEAD_DIM):
            part = total[:, head * HEAD_DIM : (head + 1) * HEAD_DIM]
            part = part * lax.rsqrt(jnp.mean(part * part, axis=-1, keepdims=True) + 1e-06)
            parts.append(part.astype(BF16))
        parts.append(total[:, width:].astype(BF16))
        rows_kv = jnp.concatenate(parts, axis=1)
        slots, count = out_ref.shape[0], rows_kv.shape[0]
        taken = lax.broadcasted_iota(jnp.int32, (slots, count), 0) == slot_ref[...]
        chosen = taken.astype(F32).astype(BF16)
        out_ref[:, : 2 * width] = jnp.dot(chosen, rows_kv, preferred_element_type=F32).astype(BF16)
        slot_sample = jnp.sum(jnp.where(taken, sample_ref[...] + 1, 0), axis=1, keepdims=True) - 1
        column = lax.broadcasted_iota(jnp.int32, (slots, HEAD_DIM), 1)
        barred = (column < 4) & (column != slot_sample)
        out_ref[:, 2 * width :] = jnp.where(barred, -PENALTY, 0.0).astype(BF16)


def text_rows(t5_all, weight_map, kv_weight, slot_of, sample, slots):
    steps, count, both = t5_all.shape
    inner, width = weight_map.shape[0] // steps, weight_map.shape[1]
    return pl.pallas_call(
        functools.partial(text_kernel, steps),
        grid=(steps,),
        out_shape=jax.ShapeDtypeStruct((slots, width + HEAD_DIM), BF16),
        in_specs=[
            pl.BlockSpec((1, count, both), lambda i: (i, 0, 0)),
            pl.BlockSpec((inner, width), lambda i: (i, 0)),
            pl.BlockSpec((both - inner, width), lambda i: (i, 0)),
            pl.BlockSpec((1, count), lambda i: (0, 0)),
            pl.BlockSpec((1, count), lambda i: (0, 0)),
        ],
        out_specs=pl.BlockSpec((slots, width + HEAD_DIM), lambda i: (0, 0)),
        scratch_shapes=[pltpu.VMEM((count, width), F32)],
        compiler_params=PARAMS,
        name="text_rows",
    )(t5_all, weight_map, kv_weight, slot_of, sample)


def prepare_kernel(lanes, lane_ref, bar_ref, *refs):
    kv_refs, key_ref, value_ref = refs[:lanes], refs[lanes], refs[lanes + 1]
    rows = kv_refs[0].shape[1]
    heads = key_ref.shape[0]
    total = lanes * rows
    ones_rows = value_ref.shape[1] - HEAD_DIM
    column = lax.broadcasted_iota(jnp.int32, (rows, HEAD_DIM), 1)
    for head in range(heads):
        key_ref[head, total:, :HEAD_DIM] = jnp.zeros((rows, HEAD_DIM), BF16)
        key_ref[head, total:, HEAD_DIM:] = jnp.where(column < 4, -PENALTY, 0.0).astype(BF16)
        value_ref[head, :HEAD_DIM, total:] = jnp.zeros((HEAD_DIM, rows), BF16)
        value_ref[head, HEAD_DIM:, :] = jnp.ones((ones_rows, total + rows), BF16)
    for shift in range(lanes):
        source = lax.rem(lane_ref[0] + lanes - shift, lanes)
        place = pl.ds(pl.multiple_of(source * rows, rows), rows)
        for head in range(heads):
            cols = pl.ds(head * HEAD_DIM, HEAD_DIM)
            key_ref[head, place, :HEAD_DIM] = kv_refs[shift][0, :, cols]
            key_ref[head, place, HEAD_DIM:] = bar_ref[place, :]
            value = kv_refs[shift][1, :, cols].astype(F32)
            value_ref[head, :HEAD_DIM, place] = value.T.astype(BF16)


def prepare(lanes, lane, barred, kv_blocks):
    rows, width = kv_blocks[0].shape[1:]
    heads, total = width // HEAD_DIM, lanes * rows + rows
    return pl.pallas_call(
        functools.partial(prepare_kernel, lanes),
        out_shape=[
            jax.ShapeDtypeStruct((heads, total, 2 * HEAD_DIM), BF16),
            jax.ShapeDtypeStruct((heads, HEAD_DIM + 16, total), BF16),
        ],
        in_specs=[SMEM] + [VMEM] * (lanes + 1),
        out_specs=[VMEM, VMEM],
        compiler_params=PARAMS,
        name="prepare",
    )(lane, barred, *kv_blocks)


def attend_kernel(lanes, shifts, info_ref, hot_ref, text_ref, key_ref, value_ref, *refs):
    count = len(shifts)
    q_refs, out_refs = refs[:count], refs[count : 2 * count]
    q_all, out_all, text_key, text_value = refs[2 * count :]
    rows, width = q_refs[0].shape
    heads = width // HEAD_DIM
    exponent_scale = math.log2(math.e) / math.sqrt(HEAD_DIM)
    for index in range(count):
        q_all[index] = q_refs[index][...]
    for head in range(heads):
        cols = pl.ds(head * HEAD_DIM, HEAD_DIM)
        text_key[head, :, :HEAD_DIM] = text_ref[:, cols]
        text_key[head, :, HEAD_DIM:] = text_ref[:, 2 * width :]
        value = text_ref[:, pl.ds(width + head * HEAD_DIM, HEAD_DIM)].astype(F32)
        text_value[head, :HEAD_DIM] = value.T.astype(BF16)
        text_value[head, HEAD_DIM:] = jnp.ones_like(text_value[head, HEAD_DIM:])

    def block(index, carry):
        shift = info_ref[1 + 2 * lanes + index]
        source = lax.rem(info_ref[0] + lanes - shift, lanes)
        hot = hot_ref[pl.ds(pl.multiple_of(source * rows, rows), rows), :]
        queries = [
            jnp.concatenate([q_all[index, :, head * HEAD_DIM : (head + 1) * HEAD_DIM], hot], axis=1)
            for head in range(heads)
        ]

        def extend(head, keys, values, largest, total):
            scores = lax.dot_general(
                keys, queries[head], (((1,), (1,)), ((), ())), preferred_element_type=F32
            )
            bound = jnp.maximum(largest, jnp.max(scores, axis=0, keepdims=True))
            weights = jnp.exp2((scores - bound) * exponent_scale).astype(BF16)
            shrink = jnp.exp2((largest - bound) * exponent_scale)
            return bound, total * shrink + jnp.dot(values, weights, preferred_element_type=F32)

        state = []
        for head in range(heads):
            largest = jnp.full((1, rows), -1e30, F32)
            total = jnp.zeros((value_ref.shape[1], rows), F32)
            state.append(extend(head, text_key[head], text_value[head], largest, total))

        first = info_ref[1 + source]

        def chunk(number, state):
            place = pl.ds(pl.multiple_of(first + number * CHUNK, 256), CHUNK)
            return [
                extend(head, key_ref[head, place, :], value_ref[head, :, place], *state[head])
                for head in range(heads)
            ]

        state = lax.fori_loop(0, info_ref[1 + lanes + source], chunk, state)
        for head in range(heads):
            total = state[head][1]
            result = total[:HEAD_DIM] / total[HEAD_DIM : HEAD_DIM + 1]
            out_all[index, :, head * HEAD_DIM : (head + 1) * HEAD_DIM] = result.T.astype(BF16)
        return carry

    lax.fori_loop(0, count, block, 0)
    for index in range(count):
        out_refs[index][...] = out_all[index]


def attend(lanes, shifts, info, hot, text, keys, values, queries):
    rows, width = queries[0].shape
    heads, count = width // HEAD_DIM, len(shifts)
    info = jnp.concatenate([info, jnp.array(shifts, jnp.int32)])
    return pl.pallas_call(
        functools.partial(attend_kernel, lanes, shifts),
        out_shape=[jax.ShapeDtypeStruct((rows, width), BF16)] * count,
        in_specs=[SMEM] + [VMEM] * (4 + count),
        out_specs=[VMEM] * count,
        scratch_shapes=[
            pltpu.VMEM((count, rows, width), BF16),
            pltpu.VMEM((count, rows, width), BF16),
            pltpu.VMEM((heads, text.shape[0], 2 * HEAD_DIM), BF16),
            pltpu.VMEM((heads, values.shape[1], text.shape[0]), BF16),
        ],
        compiler_params=PARAMS,
        name="attend",
    )(info, hot, text, keys, values, *queries)


def project_kernel(lanes, lane_ref, weight_ref, gate_ref, *refs):
    blocks, out_ref = refs[:lanes], refs[lanes]
    depth = blocks[0].shape[1]
    total = jnp.zeros(out_ref.shape, F32)
    for shift in range(lanes):
        owner = lax.rem(lane_ref[0] + shift, lanes)
        part = weight_ref[pl.ds(pl.multiple_of(owner * depth, depth), depth), :]
        total += jnp.dot(blocks[shift][...], part, preferred_element_type=F32)
    out_ref[...] = (gate_ref[...] * total).astype(BF16)


def project(lanes, lane, weight, gate_rows, blocks):
    rows, width = gate_rows.shape
    depth, tile = weight.shape[0], width // 3
    return pl.pallas_call(
        functools.partial(project_kernel, lanes),
        grid=(3,),
        out_shape=jax.ShapeDtypeStruct((rows, width), BF16),
        in_specs=[
            SMEM,
            pl.BlockSpec((depth, tile), lambda i: (0, i)),
            pl.BlockSpec((rows, tile), lambda i: (0, i)),
        ]
        + [pl.BlockSpec(blocks[0].shape, lambda i: (0, 0))] * lanes,
        out_specs=pl.BlockSpec((rows, tile), lambda i: (0, i)),
        compiler_params=PARAMS,
        name="project",
    )(lane, weight, gate_rows, *blocks)


def on_device(
    t5_attn,
    t5_out_w,
    t5_resid,
    text_dest,
    text_sample,
    kv_weight,
    img_query,
    img_key,
    img_value,
    img_sample,
    proj_weight,
    gate,
):
    groups, lanes = lax.axis_size("dp"), lax.axis_size("seq")
    group, lane = lax.axis_index("dp"), lax.axis_index("seq")
    lane_ref = lane.reshape(1)
    text_count, inner = t5_attn.shape[1:]
    capacity = 2 * text_count // groups
    rows = img_query.shape[1]
    samples = gate.shape[1]

    def shifted(block, shift):
        return lax.ppermute(block, "seq", [(i, (i + shift) % lanes) for i in range(lanes)])

    t5_all = lax.all_gather(jnp.concatenate([t5_attn[0], t5_resid[0]], axis=1), "seq")
    share = inner // groups
    own_w = lax.dynamic_slice_in_dim(t5_out_w, group * share, share, 0)
    both = jnp.concatenate([own_w, proj_weight], axis=1)
    both = lax.all_to_all(jnp.broadcast_to(both[None], (lanes,) + both.shape), "seq", 0, 0)
    w_rows = both[:, :, : own_w.shape[1]].reshape(lanes * share, -1)
    proj_rows = both[:, :, own_w.shape[1] :].reshape(lanes * proj_weight.shape[0], -1)
    kv_flat = kv_weight.reshape(kv_weight.shape[0], -1)
    own_map = jnp.dot(w_rows, kv_flat, preferred_element_type=F32).astype(BF16)
    map_all = lax.all_to_all(jnp.broadcast_to(own_map[None], (groups,) + own_map.shape), "dp", 0, 0)
    map_all = map_all.reshape(groups, lanes, share, -1).transpose(1, 0, 2, 3).reshape(lanes * inner, -1)
    projection = lax.all_gather(proj_rows, "dp", axis=0, tiled=True)

    target = text_dest[0, :, 0]
    order = jnp.arange(text_count, dtype=jnp.int32)
    ahead = (target[None, :] == target[:, None]) & (order[:, None] < order[None, :])
    slot_of = target * capacity + jnp.sum(ahead.astype(jnp.int32), axis=0)

    sample = img_sample[0]
    column = jnp.arange(HEAD_DIM, dtype=jnp.int32)[None, :]
    hot = (sample[:, None] == column).astype(BF16)
    barred = jnp.where((column < samples) & (sample[:, None] != column), -PENALTY, 0.0).astype(BF16)
    ends = sample.reshape(lanes, rows)
    low = jnp.sum((sample[None, :] < ends[:, :1]).astype(jnp.int32), axis=1) // 256 * 256
    high = jnp.sum((sample[None, :] <= ends[:, -1:]).astype(jnp.int32), axis=1)
    info = jnp.concatenate([lane_ref, low, (high - low + CHUNK - 1) // CHUNK]).astype(jnp.int32)

    packed = pack(lanes, lane_ref, img_query[0], img_key[0], img_value[0])
    kv_out, q_out = packed[:lanes], packed[lanes:]
    order = (4, 3, 5, 2, 6, 1, 7)
    kv_in, q_in = {0: kv_out[0]}, {0: q_out[0]}
    for shift in order:
        kv_in[shift] = shifted(kv_out[shift], shift)
    for shift in order:
        q_in[shift] = shifted(q_out[shift], shift)

    sent = text_rows(t5_all, map_all, kv_flat, slot_of[None], text_sample, groups * capacity)
    text = lax.all_to_all(sent.reshape(groups, capacity, -1), "dp", 0, 0).reshape(sent.shape)

    keys, values = prepare(lanes, lane_ref, barred, [kv_in[s] for s in range(lanes)])
    returned = {}
    for shifts in SHIFT_GROUPS:
        results = attend(lanes, shifts, info, hot, text, keys, values, [q_in[s] for s in shifts])
        for shift, result in zip(shifts, results):
            returned[shift] = shifted(result, -shift) if shift else result

    own_sample = lax.dynamic_slice_in_dim(sample, lane * rows, rows)
    gate_rows = jnp.zeros((rows, gate.shape[2]), F32)
    for number in range(samples):
        gate_rows = jnp.where(own_sample[:, None] == number, gate[0, number][None, :], gate_rows)
    out = project(lanes, lane_ref, projection, gate_rows, [returned[s] for s in range(lanes)])
    return out[None]


SHIFT_GROUPS = ((4, 3, 5, 2, 6, 1, 7, 0),)


def solution(mesh):
    placed = (
        P("dp", None, "seq"),
        P("seq", None),
        P("dp", None, "seq"),
        P("dp", None, None),
        P("dp", None),
        P(None, None, "seq"),
        P("dp", "seq", None),
        P("dp", "seq", None),
        P("dp", "seq", None),
        P("dp", None),
        P(("dp", "seq"), None),
        P("dp", None, None),
    )
    return jax.shard_map(
        on_device, mesh=mesh, in_specs=placed, out_specs=P("dp", "seq", None), check_vma=False
    )
```

time: 331 us -> 357 us (1.079); the launches traced: 324 us -> 356 us
  Pallas kernels: 0 us -> 143 us
  waiting for transfers between devices: 149 us -> 59.1 us
  matrix products: 54.4 us -> 0.83 us
  blocking collectives: 0 us -> 35.6 us
  starting transfers between devices: 36.1 us -> 59.9 us
  local copies, waits for them, and re-layouts: 52.4 us -> 36.2 us
  other arithmetic: 16.9 us -> 7.78 us
    pallas_call x0 -> x5, Pallas kernels: none -> 143 us  [the longest x1 96.6 us: pack(): pl.pallas_call(functools.partial(pack_kernel, lanes), out_shape=[jax.Shap...]
    all_to_all x6 -> x2, waiting for transfers between devices: 92.4 us -> 0.01 us  [the longest x1 0.01 us: on_device(): lax.all_to_all(jnp.broadcast_to(own_map[None], (groups,) + own_map.shape)...]
    ppermute x0 -> x21, waiting for transfers between devices: none -> 59.1 us  [shifted(): lax.ppermute(block, 'seq', [(i, (i + shift) % lanes) for i in range(lanes)])]
    psum x1 -> x0, waiting for transfers between devices: 56.3 us -> none  [on_device(): t5_layer = lax.psum(t5_term, 'seq').astype(jnp.float32).astype(jnp.bfloat16)]
    ppermute x0 -> x21, starting transfers between devices: none -> 45 us  [shifted(): lax.ppermute(block, 'seq', [(i, (i + shift) % lanes) for i in range(lanes)])]
    all_to_all x0 -> x1, blocking collectives: none -> 35.6 us  [on_device(): lax.all_to_all(jnp.broadcast_to(both[None], (lanes,) + both.shape), 'seq'...]
    dot_general x7 -> x1, matrix products: 35.7 us -> 0.83 us  [on_device(): own_map = jnp.dot(w_rows, kv_flat, preferred_element_type=F32).astype(BF16)]
    all_to_all x6 -> x2, starting transfers between devices: 36.1 us -> 14.9 us  [the longest x1 7.49 us: on_device(): lax.all_to_all(jnp.broadcast_to(own_map[None], (groups,) + own_map.shape)...]
  transfers between devices with their start and end apart: 8 -> 25, of which waited for: 6 -> 10; matrix products, arithmetic and copies ran while one was open for 34% -> 5% of each run, Pallas kernels for 0% -> 39%
where the time goes in v1:
time: 357 us; the launch traced here: 356 us
  Pallas kernels  143 us (40%)
  starting transfers between devices  59.9 us (17%)
  waiting for transfers between devices  59.1 us (17%)
  local copies, waits for them, and re-layouts  36.2 us (10%)
  blocking collectives  35.6 us (10%)
  between operations  13.6 us (4%)
  other arithmetic  7.78 us (2%)
    pallas_call x1, Pallas kernels, pack(): pl.pallas_call(functools.partial(pack_kernel, lanes), out_shape=[jax.Shap...  96.6 us
    ppermute x21, waiting for transfers between devices, shifted(): lax.ppermute(block, 'seq', [(i, (i + shift) % lanes) for i in range(lanes)])  59.1 us
    ppermute x21, starting transfers between devices, shifted(): lax.ppermute(block, 'seq', [(i, (i + shift) % lanes) for i in range(lanes)])  45 us
    all_to_all x1, blocking collectives, on_device(): lax.all_to_all(jnp.broadcast_to(both[None], (lanes,) + both.shape), 'seq'...  35.6 us
    pallas_call x1, Pallas kernels, attend(): pl.pallas_call(functools.partial(attend_kernel, lanes, shifts), out_shape...  31.9 us
    unnamed x78, local copies, waits for them, and re-layouts  30.1 us
    all_to_all x1, starting transfers between devices, on_device(): lax.all_to_all(jnp.broadcast_to(own_map[None], (groups,) + own_map.shape)...  7.49 us
    all_to_all x1, starting transfers between devices, on_device(): lax.all_to_all(sent.reshape(groups, capacity, -1), 'dp', 0, 0)  7.38 us
  transfers between devices with their start and end apart: 25, of which 10 were waited for; matrix products, arithmetic and copies ran while one was open for 5% of the time, Pallas kernels for 39%

profile of v1, /device:TPU:20, one launch (start us, length us, event | category | flops | bytes accessed | tf_op | source)
XLA Modules:
  0.0 356.5 jit_solution(12383153773408277463)
XLA Ops:
  9.2 35.6 %all_to_all.15 = bf16[8,8,5632]{2,1,0:T(8,128)(2,1)S(1)} all-to-all(bf16[8,8,5632]{2,1,0:T(8,128)(2,1)S(1)} %broadcast_in_dim.88), channel_id=1, replica_groups=mesh['dp'=32,'seq'=8] {'seq'}, dimensions={0} | all-to-all | bytes 1441792 | tf_op jit(solution)/shard_map/all_to_all | solution.py:287
  45.5 3.0 copy.24
  52.1 7.5 %all-to-all-start.1 = ((bf16[32,64,512]{2,1,0:T(8,128)(2,1)}), bf16[32,64,512]{2,1,0:T(8,128)(2,1)}, u32[]{:S(2)}, u32[]{:S(2)}) async-start(bf16[32,64,512]{2,1,0:T(8,128)(2,1)} %broadcast_in_dim.102), calls=%async_computation.1 | async-start | bytes 4194304 | tf_op jit(solution)/shard_map/all_to_all | solution.py:292
  59.6 96.6 %pack.1 = (bf16[2,256,256]{2,1,0:T(8,128)(2,1)}, bf16[2,256,256]{2,1,0:T(8,128)(2,1)}, bf16[2,256,256]{2,1,0:T(8,128)(2,1)}, bf16[2,256,256]{2,1,0:T(8,128)(2,1)...) custom-call(s32[1]{0:T(128)} %bitcast.lane_ref, ...), custom_call_target="tpu_custom_call" | custom-call | tf_op jit(solution)/shard_map/pack/pallas_call | solution.py:42
  156.9 2.4 collective-permute-start.2
  159.3 4.1 %collective-permute-start.10 = (bf16[256,256]{1,0:T(8,128)(2,1)}, bf16[256,256]{1,0:T(8,128)(2,1)S(1)}, u32[]{:S(2)}, u32[]{:S(2)}) collective-permute-start(bf16[256,256]{1,0:T(8,128)(2,1)} %get-tuple-element.44), channel_id=1, source_target_pairs={{0,2},{1,3},{2,4},{3,5},{4,6},{5,7},{6,0},{7,1},{8,10},{9,11},{10,... | collective-permute-start | bytes 393224 | tf_op jit(solution)/shard_map/ppermute | solution.py:281
  168.2 28.7 %collective-permute-done.10.refs_3_ = bf16[256,256]{1,0:T(8,128)(2,1)S(1)} collective-permute-done((bf16[256,256]{1,0:T(8,128)(2,1)}, bf16[256,256]{1,0:T(8,128)(2,1)S(1)}, u32[]{:S(2)}, u32[]{:S(2)}) %collective-permute-start.10) | collective-permute-done | bytes 131104 | tf_op jit(solution)/shard_map/ppermute | solution.py:281
  196.9 3.1 collective-permute-start.3
  200.1 5.7 %collective-permute-start.4 = (bf16[2,256,256]{2,1,0:T(8,128)(2,1)}, bf16[2,256,256]{2,1,0:T(8,128)(2,1)}, u32[]{:S(2)}, u32[]{:S(2)}) collective-permute-start(bf16[2,256,256]{2,1,0:T(8,128)(2,1)} %get-tuple-element.36), channel_id=1, source_target_pairs={{0,5},{1,6},{2,7},{3,0},{4,1},{5,2},{6,3},{7,4},{8,13},{9,14},{10,... | collective-permute-start | bytes 786440 | tf_op jit(solution)/shard_map/ppermute | solution.py:281
  207.9 3.1 copy.21
  214.1 6.0 %text_rows.1 = bf16[256,640]{1,0:T(8,128)(2,1)S(1)} custom-call(bf16[8,128,768]{2,1,0:T(8,128)(2,1)S(1)} %bitcast.31, bf16[2048,512]{1,0:T(8,128)(2,1)S(1)} %bitcast.30, bf16[4096,512]{1,0:T(8,128)(2,1)} %bitcast.35, s32[1,128]{1,0:T(1,128)S(1)} %bitcast_add_fusion.slot_ref, s32[1,128]{1,0:T(1,128)S(1)} %copy-done.25), custom_call_target="tpu_custom_call" | custom-call | tf_op jit(solution)/shard_map/text_rows/pallas_call | solution.py:89
  220.8 7.4 %all-to-all-start.2 = ((bf16[32,8,640]{2,1,0:T(8,128)(2,1)}), bf16[32,8,640]{2,1,0:T(8,128)(2,1)S(1)}, u32[]{:S(2)}, u32[]{:S(2)}) async-start(bf16[32,8,640]{2,1,0:T(8,128)(2,1)} %bitcast.33), calls=%async_computation.2 | async-start | bytes 655360 | tf_op jit(solution)/shard_map/all_to_all | solution.py:320
  231.8 3.2 collective-permute-start.7
  235.0 7.0 %collective-permute-done.5.refs_6_ = bf16[2,256,256]{2,1,0:T(8,128)(2,1)} collective-permute-done((bf16[2,256,256]{2,1,0:T(8,128)(2,1)}, bf16[2,256,256]{2,1,0:T(8,128)(2,1)}, u32[]{:S(2)}, u32[]{:S(2)}) %collective-permute-start.5) | collective-permute-done | bytes 262176 | tf_op jit(solution)/shard_map/ppermute | solution.py:281
  242.0 4.1 %collective-permute-start.8 = (bf16[256,256]{1,0:T(8,128)(2,1)}, bf16[256,256]{1,0:T(8,128)(2,1)S(1)}, u32[]{:S(2)}, u32[]{:S(2)}) collective-permute-start(bf16[256,256]{1,0:T(8,128)(2,1)} %get-tuple-element.42), channel_id=1, source_target_pairs={{0,3},{1,4},{2,5},{3,6},{4,7},{5,0},{6,1},{7,2},{8,11},{9,12},{10,... | collective-permute-start | bytes 393224 | tf_op jit(solution)/shard_map/ppermute | solution.py:281
  251.8 3.4 prepare.1
  258.9 3.0 collective-permute-done.9.refs_2_
  270.2 31.9 %attend.1 = (bf16[256,256]{1,0:T(8,128)(2,1)S(1)}, bf16[256,256]{1,0:T(8,128)(2,1)S(1)}, bf16[256,256]{1,0:T(8,128)(2,1)S(1)}, bf16[256,256]{1,0:T(8,128)(2,1)},...) custom-call(s32[25]{0:T(128)S(1)} %pad_add_fusion.info_ref, ...), custom_call_target="tpu_custom_call" | custom-call | tf_op jit(solution)/shard_map/attend/pallas_call | solution.py:212
  306.0 5.2 %collective-permute-start.14 = (bf16[256,256]{1,0:T(8,128)(2,1)}, bf16[256,256]{1,0:T(8,128)(2,1)S(1)}, u32[]{:S(2)}, u32[]{:S(2)}) collective-permute-start(bf16[256,256]{1,0:T(8,128)(2,1)} %get-tuple-element.50), channel_id=1, source_target_pairs={{0,7},{1,0},{2,1},{3,2},{4,3},{5,4},{6,5},{7,6},{8,15},{9,8},{10,9... | collective-permute-start | bytes 393224 | tf_op jit(solution)/shard_map/ppermute | solution.py:281
  311.3 4.3 %collective-permute-start.16 = (bf16[256,256]{1,0:T(8,128)(2,1)}, bf16[256,256]{1,0:T(8,128)(2,1)S(1)}, u32[]{:S(2)}, u32[]{:S(2)}) collective-permute-start(bf16[256,256]{1,0:T(8,128)(2,1)} %copy-done.30), channel_id=1, source_target_pairs={{0,5},{1,6},{2,7},{3,0},{4,1},{5,2},{6,3},{7,4},{8,13},{9,14},{10,... | collective-permute-start | bytes 393224 | tf_op jit(solution)/shard_map/ppermute | solution.py:281
  319.4 2.7 collective-permute-start.19
  325.7 9.2 %collective-permute-done.16.refs_3_ = bf16[256,256]{1,0:T(8,128)(2,1)S(1)} collective-permute-done((bf16[256,256]{1,0:T(8,128)(2,1)}, bf16[256,256]{1,0:T(8,128)(2,1)S(1)}, u32[]{:S(2)}, u32[]{:S(2)}) %collective-permute-start.16) | collective-permute-done | bytes 131104 | tf_op jit(solution)/shard_map/ppermute | solution.py:281
  335.5 5.5 %collective-permute-done.19.refs_6_ = bf16[256,256]{1,0:T(8,128)(2,1)S(1)} collective-permute-done((bf16[256,256]{1,0:T(8,128)(2,1)}, bf16[256,256]{1,0:T(8,128)(2,1)S(1)}, u32[]{:S(2)}, u32[]{:S(2)}) %collective-permute-start.19) | collective-permute-done | bytes 131104 | tf_op jit(solution)/shard_map/ppermute | solution.py:281
  344.2 5.4 %project.1 = bf16[256,1536]{1,0:T(8,128)(2,1)} custom-call(s32[1]{0:T(128)} %bitcast.lane_ref, bf16[2048,1536]{1,0:T(8,128)(2,1)} %all-gather.4.cloned.1.call-done.weight_ref, f32[256,1536]{1,0:T(8,128)S(1)} %copy-done.2, bf16[256,256]{1,0:T(8,128)(2,1)S(1)} %copy-done.11, bf16[256,256]{1,0:T(8,128)(2,1)S(1)} %collective-permute-done.14.refs_1_, ...), custom_call_target="tpu_custom_call" | custom-call | tf_op jit(solution)/shard_map/project/pallas_call | solution.py:242
  (134 shorter events, 54.6 us)
Async XLA Ops:
  6.5 204.5 %all-gather.6.cloned.1.call-start = ((), (), s32[]{:S(2)}) async-start(), calls=%async_computation.4 | async-start | bytes 1769472 | tf_op jit(solution)/shard_map/all_gather | solution.py:283
  8.3 333.6 %all-gather.4.cloned.1.call-start = ((), (), s32[]{:S(2)}) async-start(), calls=%async_computation.3 | async-start | bytes 6488064 | tf_op jit(solution)/shard_map/all_gather | solution.py:294
  52.1 155.8 %all-to-all-start.1 = ((bf16[32,64,512]{2,1,0:T(8,128)(2,1)}), bf16[32,64,512]{2,1,0:T(8,128)(2,1)}, u32[]{:S(2)}, u32[]{:S(2)}) async-start(bf16[32,64,512]{2,1,0:T(8,128)(2,1)} %broadcast_in_dim.102), calls=%async_computation.1 | async-start | bytes 4194304 | tf_op jit(solution)/shard_map/all_to_all | solution.py:292
  156.3 49.5 %collective-permute-start = (bf16[2,256,256]{2,1,0:T(8,128)(2,1)}, bf16[2,256,256]{2,1,0:T(8,128)(2,1)S(1)}, u32[]{:S(2)}, u32[]{:S(2)}) collective-permute-start(bf16[2,256,256]{2,1,0:T(8,128)(2,1)} %get-tuple-element.32), channel_id=1, source_target_pairs={{0,1},{1,2},{2,3},{3,4},{4,5},{5,6},{6,7},{7,0},{8,9},{9,10},{10,1... | collective-permute-start | bytes 786440 | tf_op jit(solution)/shard_map/ppermute | solution.py:281
  156.7 49.0 %collective-permute-start.1 = (bf16[2,256,256]{2,1,0:T(8,128)(2,1)}, bf16[2,256,256]{2,1,0:T(8,128)(2,1)}, u32[]{:S(2)}, u32[]{:S(2)}) collective-permute-start(bf16[2,256,256]{2,1,0:T(8,128)(2,1)} %get-tuple-element.33), channel_id=1, source_target_pairs={{0,2},{1,3},{2,4},{3,5},{4,6},{5,7},{6,0},{7,1},{8,10},{9,11},{10,... | collective-permute-start | bytes 786440 | tf_op jit(solution)/shard_map/ppermute | solution.py:281
  156.9 71.4 %collective-permute-start.2 = (bf16[2,256,256]{2,1,0:T(8,128)(2,1)}, bf16[2,256,256]{2,1,0:T(8,128)(2,1)}, u32[]{:S(2)}, u32[]{:S(2)}) collective-permute-start(bf16[2,256,256]{2,1,0:T(8,128)(2,1)} %get-tuple-element.34), channel_id=1, source_target_pairs={{0,3},{1,4},{2,5},{3,6},{4,7},{5,0},{6,1},{7,2},{8,11},{9,12},{10,... | collective-permute-start | bytes 786440 | tf_op jit(solution)/shard_map/ppermute | solution.py:281
  159.3 37.6 %collective-permute-start.10 = (bf16[256,256]{1,0:T(8,128)(2,1)}, bf16[256,256]{1,0:T(8,128)(2,1)S(1)}, u32[]{:S(2)}, u32[]{:S(2)}) collective-permute-start(bf16[256,256]{1,0:T(8,128)(2,1)} %get-tuple-element.44), channel_id=1, source_target_pairs={{0,2},{1,3},{2,4},{3,5},{4,6},{5,7},{6,0},{7,1},{8,10},{9,11},{10,... | collective-permute-start | bytes 393224 | tf_op jit(solution)/shard_map/ppermute | solution.py:281
  163.4 36.7 %collective-permute-start.11 = (bf16[256,256]{1,0:T(8,128)(2,1)}, bf16[256,256]{1,0:T(8,128)(2,1)}, u32[]{:S(2)}, u32[]{:S(2)}) collective-permute-start(bf16[256,256]{1,0:T(8,128)(2,1)} %get-tuple-element.45), channel_id=1, source_target_pairs={{0,6},{1,7},{2,0},{3,1},{4,2},{5,3},{6,4},{7,5},{8,14},{9,15},{10,... | collective-permute-start | bytes 393224 | tf_op jit(solution)/shard_map/ppermute | solution.py:281
  196.9 32.9 %collective-permute-start.3 = (bf16[2,256,256]{2,1,0:T(8,128)(2,1)}, bf16[2,256,256]{2,1,0:T(8,128)(2,1)}, u32[]{:S(2)}, u32[]{:S(2)}) collective-permute-start(bf16[2,256,256]{2,1,0:T(8,128)(2,1)} %get-tuple-element.35), channel_id=1, source_target_pairs={{0,4},{1,5},{2,6},{3,7},{4,0},{5,1},{6,2},{7,3},{8,12},{9,13},{10,... | collective-permute-start | bytes 786440 | tf_op jit(solution)/shard_map/ppermute | solution.py:281
  200.1 31.7 %collective-permute-start.4 = (bf16[2,256,256]{2,1,0:T(8,128)(2,1)}, bf16[2,256,256]{2,1,0:T(8,128)(2,1)}, u32[]{:S(2)}, u32[]{:S(2)}) collective-permute-start(bf16[2,256,256]{2,1,0:T(8,128)(2,1)} %get-tuple-element.36), channel_id=1, source_target_pairs={{0,5},{1,6},{2,7},{3,0},{4,1},{5,2},{6,3},{7,4},{8,13},{9,14},{10,... | collective-permute-start | bytes 786440 | tf_op jit(solution)/shard_map/ppermute | solution.py:281
  205.8 36.3 %collective-permute-start.5 = (bf16[2,256,256]{2,1,0:T(8,128)(2,1)}, bf16[2,256,256]{2,1,0:T(8,128)(2,1)}, u32[]{:S(2)}, u32[]{:S(2)}) collective-permute-start(bf16[2,256,256]{2,1,0:T(8,128)(2,1)} %get-tuple-element.37), channel_id=1, source_target_pairs={{0,6},{1,7},{2,0},{3,1},{4,2},{5,3},{6,4},{7,5},{8,14},{9,15},{10,... | collective-permute-start | bytes 786440 | tf_op jit(solution)/shard_map/ppermute | solution.py:281
  205.8 42.3 %collective-permute-start.6 = (bf16[2,256,256]{2,1,0:T(8,128)(2,1)}, bf16[2,256,256]{2,1,0:T(8,128)(2,1)}, u32[]{:S(2)}, u32[]{:S(2)}) collective-permute-start(bf16[2,256,256]{2,1,0:T(8,128)(2,1)} %get-tuple-element.38), channel_id=1, source_target_pairs={{0,7},{1,0},{2,1},{3,2},{4,3},{5,4},{6,5},{7,6},{8,15},{9,8},{10,9... | collective-permute-start | bytes 786440 | tf_op jit(solution)/shard_map/ppermute | solution.py:281
  220.8 41.7 %all-to-all-start.2 = ((bf16[32,8,640]{2,1,0:T(8,128)(2,1)}), bf16[32,8,640]{2,1,0:T(8,128)(2,1)S(1)}, u32[]{:S(2)}, u32[]{:S(2)}) async-start(bf16[32,8,640]{2,1,0:T(8,128)(2,1)} %bitcast.33), calls=%async_computation.2 | async-start | bytes 655360 | tf_op jit(solution)/shard_map/all_to_all | solution.py:320
  228.2 28.0 %collective-permute-start.12 = (bf16[256,256]{1,0:T(8,128)(2,1)}, bf16[256,256]{1,0:T(8,128)(2,1)S(1)}, u32[]{:S(2)}, u32[]{:S(2)}) collective-permute-start(bf16[256,256]{1,0:T(8,128)(2,1)} %get-tuple-element.46), channel_id=1, source_target_pairs={{0,1},{1,2},{2,3},{3,4},{4,5},{5,6},{6,7},{7,0},{8,9},{9,10},{10,1... | collective-permute-start | bytes 393224 | tf_op jit(solution)/shard_map/ppermute | solution.py:281
  229.8 27.1 %collective-permute-start.13 = (bf16[256,256]{1,0:T(8,128)(2,1)}, bf16[256,256]{1,0:T(8,128)(2,1)S(1)}, u32[]{:S(2)}, u32[]{:S(2)}) collective-permute-start(bf16[256,256]{1,0:T(8,128)(2,1)} %get-tuple-element.47), channel_id=1, source_target_pairs={{0,7},{1,0},{2,1},{3,2},{4,3},{5,4},{6,5},{7,6},{8,15},{9,8},{10,9... | collective-permute-start | bytes 393224 | tf_op jit(solution)/shard_map/ppermute | solution.py:281
  231.8 25.8 %collective-permute-start.7 = (bf16[256,256]{1,0:T(8,128)(2,1)}, bf16[256,256]{1,0:T(8,128)(2,1)S(1)}, u32[]{:S(2)}, u32[]{:S(2)}) collective-permute-start(bf16[256,256]{1,0:T(8,128)(2,1)} %get-tuple-element.41), channel_id=1, source_target_pairs={{0,4},{1,5},{2,6},{3,7},{4,0},{5,1},{6,2},{7,3},{8,12},{9,13},{10,... | collective-permute-start | bytes 393224 | tf_op jit(solution)/shard_map/ppermute | solution.py:281
  242.0 16.2 %collective-permute-start.8 = (bf16[256,256]{1,0:T(8,128)(2,1)}, bf16[256,256]{1,0:T(8,128)(2,1)S(1)}, u32[]{:S(2)}, u32[]{:S(2)}) collective-permute-start(bf16[256,256]{1,0:T(8,128)(2,1)} %get-tuple-element.42), channel_id=1, source_target_pairs={{0,3},{1,4},{2,5},{3,6},{4,7},{5,0},{6,1},{7,2},{8,11},{9,12},{10,... | collective-permute-start | bytes 393224 | tf_op jit(solution)/shard_map/ppermute | solution.py:281
  248.1 13.8 %collective-permute-start.9 = (bf16[256,256]{1,0:T(8,128)(2,1)}, bf16[256,256]{1,0:T(8,128)(2,1)S(1)}, u32[]{:S(2)}, u32[]{:S(2)}) collective-permute-start(bf16[256,256]{1,0:T(8,128)(2,1)} %get-tuple-element.43), channel_id=1, source_target_pairs={{0,5},{1,6},{2,7},{3,0},{4,1},{5,2},{6,3},{7,4},{8,13},{9,14},{10,... | collective-permute-start | bytes 393224 | tf_op jit(solution)/shard_map/ppermute | solution.py:281
  306.0 13.4 %collective-permute-start.14 = (bf16[256,256]{1,0:T(8,128)(2,1)}, bf16[256,256]{1,0:T(8,128)(2,1)S(1)}, u32[]{:S(2)}, u32[]{:S(2)}) collective-permute-start(bf16[256,256]{1,0:T(8,128)(2,1)} %get-tuple-element.50), channel_id=1, source_target_pairs={{0,7},{1,0},{2,1},{3,2},{4,3},{5,4},{6,5},{7,6},{8,15},{9,8},{10,9... | collective-permute-start | bytes 393224 | tf_op jit(solution)/shard_map/ppermute | solution.py:281
  311.3 23.6 %collective-permute-start.16 = (bf16[256,256]{1,0:T(8,128)(2,1)}, bf16[256,256]{1,0:T(8,128)(2,1)S(1)}, u32[]{:S(2)}, u32[]{:S(2)}) collective-permute-start(bf16[256,256]{1,0:T(8,128)(2,1)} %copy-done.30), channel_id=1, source_target_pairs={{0,5},{1,6},{2,7},{3,0},{4,1},{5,2},{6,3},{7,4},{8,13},{9,14},{10,... | collective-permute-start | bytes 393224 | tf_op jit(solution)/shard_map/ppermute | solution.py:281
  315.7 19.2 %collective-permute-start.17 = (bf16[256,256]{1,0:T(8,128)(2,1)}, bf16[256,256]{1,0:T(8,128)(2,1)S(1)}, u32[]{:S(2)}, u32[]{:S(2)}) collective-permute-start(bf16[256,256]{1,0:T(8,128)(2,1)} %copy-done.29), channel_id=1, source_target_pairs={{0,4},{1,5},{2,6},{3,7},{4,0},{5,1},{6,2},{7,3},{8,12},{9,13},{10,... | collective-permute-start | bytes 393224 | tf_op jit(solution)/shard_map/ppermute | solution.py:281
  317.4 18.2 %collective-permute-start.18 = (bf16[256,256]{1,0:T(8,128)(2,1)}, bf16[256,256]{1,0:T(8,128)(2,1)S(1)}, u32[]{:S(2)}, u32[]{:S(2)}) collective-permute-start(bf16[256,256]{1,0:T(8,128)(2,1)} %copy-done.28), channel_id=1, source_target_pairs={{0,3},{1,4},{2,5},{3,6},{4,7},{5,0},{6,1},{7,2},{8,11},{9,12},{10,... | collective-permute-start | bytes 393224 | tf_op jit(solution)/shard_map/ppermute | solution.py:281
  319.4 21.6 %collective-permute-start.19 = (bf16[256,256]{1,0:T(8,128)(2,1)}, bf16[256,256]{1,0:T(8,128)(2,1)S(1)}, u32[]{:S(2)}, u32[]{:S(2)}) collective-permute-start(bf16[256,256]{1,0:T(8,128)(2,1)} %copy-done.27), channel_id=1, source_target_pairs={{0,2},{1,3},{2,4},{3,5},{4,6},{5,7},{6,0},{7,1},{8,10},{9,11},{10,... | collective-permute-start | bytes 393224 | tf_op jit(solution)/shard_map/ppermute | solution.py:281
  324.1 17.8 %collective-permute-start.20 = (bf16[256,256]{1,0:T(8,128)(2,1)}, bf16[256,256]{1,0:T(8,128)(2,1)S(1)}, u32[]{:S(2)}, u32[]{:S(2)}) collective-permute-start(bf16[256,256]{1,0:T(8,128)(2,1)} %copy-done.26), channel_id=1, source_target_pairs={{0,1},{1,2},{2,3},{3,4},{4,5},{5,6},{6,7},{7,0},{8,9},{9,10},{10,1... | collective-permute-start | bytes 393224 | tf_op jit(solution)/shard_map/ppermute | solution.py:281
  (38 other events, 315.8 us)
Sparse Core Ops, SparseCore 0:
  9.1 49.1 all-gather.5
  60.9 54.9 all-gather.3

commit v2 on v1

v2 whole, which is shorter than its diff:
```python
import functools
import math

import jax
import jax.numpy as jnp
from jax import lax
from jax.experimental import pallas as pl
from jax.experimental.pallas import tpu as pltpu
from jax.sharding import PartitionSpec as P

HEAD_DIM = 128
PENALTY = 524288.0
CHUNK = 1024
ALIGN = 256
BF16 = jnp.bfloat16
F32 = jnp.float32
VMEM = pl.BlockSpec(memory_space=pltpu.VMEM)
SMEM = pl.BlockSpec(memory_space=pltpu.SMEM)
ANY = pl.BlockSpec(memory_space=pl.ANY)
PARAMS = pltpu.CompilerParams(vmem_limit_bytes=60 * 1024 * 1024)


def whole(array):
    zeros = (0,) * len(array.shape)
    return pl.BlockSpec(array.shape, lambda i: zeros)


def cost(microseconds):
    return pl.CostEstimate(flops=int(microseconds * 1.1e9), bytes_accessed=0, transcendentals=0)


def pack_kernel(lanes, lane_ref, *refs):
    sources = len(refs) - lanes
    width = refs[0].shape[1] // lanes
    for shift in range(lanes):
        owner = lax.rem(lane_ref[0] + shift, lanes)
        cols = pl.ds(pl.multiple_of(owner * width, width), width)
        for index in range(sources):
            refs[sources + shift][index] = refs[index][:, cols]


def pack(lanes, lane, *arrays):
    rows, features = arrays[0].shape
    out = jax.ShapeDtypeStruct((len(arrays), rows, features // lanes), arrays[0].dtype)
    return pl.pallas_call(
        functools.partial(pack_kernel, lanes),
        grid=(1,),
        out_shape=[out] * lanes,
        in_specs=[SMEM] + [whole(a) for a in arrays],
        out_specs=[whole(out)] * lanes,
        compiler_params=PARAMS,
        cost_estimate=cost(2),
        name="pack",
    )(lane, *arrays)


def text_kernel(steps, lane_ref, t5_ref, map_ref, kvw_ref, slot_ref, sample_ref, out_ref, total):
    step = pl.program_id(0)
    inner = map_ref.shape[0]

    @pl.when(step == 0)
    def _():
        total[...] = jnp.zeros_like(total)

    rows = t5_ref[0]
    total[...] += jnp.dot(rows[:, :inner], map_ref[...], preferred_element_type=F32) + jnp.dot(
        rows[:, inner:], kvw_ref[...], preferred_element_type=F32
    )

    @pl.when(step == steps - 1)
    def _():
        width = total.shape[1] // 2
        parts = []
        for head in range(width // HEAD_DIM):
            part = total[:, head * HEAD_DIM : (head + 1) * HEAD_DIM]
            part = part * lax.rsqrt(jnp.mean(part * part, axis=-1, keepdims=True) + 1e-06)
            parts.append(part.astype(BF16))
        parts.append(total[:, width:].astype(BF16))
        rows_kv = jnp.concatenate(parts, axis=1)
        slots, count = out_ref.shape[0], rows_kv.shape[0]
        taken = lax.broadcasted_iota(jnp.int32, (slots, count), 0) == slot_ref[...]
        chosen = taken.astype(F32).astype(BF16)
        out_ref[:, : 2 * width] = jnp.dot(chosen, rows_kv, preferred_element_type=F32).astype(BF16)
        slot_sample = jnp.sum(jnp.where(taken, sample_ref[...] + 1, 0), axis=1, keepdims=True) - 1
        column = lax.broadcasted_iota(jnp.int32, (slots, HEAD_DIM), 1)
        barred = (column < 4) & (column != slot_sample)
        out_ref[:, 2 * width :] = jnp.where(barred, -PENALTY, 0.0).astype(BF16)


def text_rows(lane, t5_all, weight_map, kv_weight, slot_of, sample, slots):
    steps, count, both = t5_all.shape
    inner, width = weight_map.shape[0] // steps, weight_map.shape[1]

    def source(i, lane_ref):
        return lax.rem(lane_ref[0] + steps - i, steps)

    return pl.pallas_call(
        functools.partial(text_kernel, steps),
        grid_spec=pltpu.PrefetchScalarGridSpec(
            num_scalar_prefetch=1,
            grid=(steps,),
            in_specs=[
                pl.BlockSpec((1, count, both), lambda i, lane_ref: (source(i, lane_ref), 0, 0)),
                pl.BlockSpec((inner, width), lambda i, lane_ref: (i, 0)),
                pl.BlockSpec((both - inner, width), lambda i, lane_ref: (source(i, lane_ref), 0)),
                pl.BlockSpec((1, count), lambda i, lane_ref: (0, 0)),
                pl.BlockSpec((1, count), lambda i, lane_ref: (0, 0)),
            ],
            out_specs=pl.BlockSpec((slots, width + HEAD_DIM), lambda i, lane_ref: (0, 0)),
            scratch_shapes=[pltpu.VMEM((count, width), F32)],
        ),
        out_shape=jax.ShapeDtypeStruct((slots, width + HEAD_DIM), BF16),
        compiler_params=PARAMS,
        cost_estimate=cost(5),
        name="text_rows",
    )(lane, t5_all, weight_map, kv_weight, slot_of, sample)


def prepare_kernel(lanes, lane_ref, bar_ref, *refs):
    kv_refs, key_ref, value_ref = refs[:lanes], refs[lanes], refs[lanes + 1]
    rows = kv_refs[0].shape[1]
    heads, _, extent = key_ref.shape
    total = lanes * rows
    feature = lax.broadcasted_iota(jnp.int32, (HEAD_DIM, extent - total), 0)
    for head in range(heads):
        key_ref[head, :HEAD_DIM, total:] = jnp.zeros((HEAD_DIM, extent - total), BF16)
        key_ref[head, HEAD_DIM:, total:] = jnp.where(feature < 4, -PENALTY, 0.0).astype(BF16)
        value_ref[head, total:, :HEAD_DIM] = jnp.zeros((extent - total, HEAD_DIM), BF16)
        value_ref[head, :, HEAD_DIM:] = jnp.ones((extent, HEAD_DIM), BF16)
    for shift in range(lanes):
        source = lax.rem(lane_ref[0] + lanes - shift, lanes)
        place = pl.ds(pl.multiple_of(source * rows, rows), rows)
        barred = bar_ref[place, :].astype(F32).T.astype(BF16)
        for head in range(heads):
            cols = pl.ds(head * HEAD_DIM, HEAD_DIM)
            key_ref[head, :HEAD_DIM, place] = kv_refs[shift][0, :, cols].astype(F32).T.astype(BF16)
            key_ref[head, HEAD_DIM:, place] = barred
            value_ref[head, place, :HEAD_DIM] = kv_refs[shift][1, :, cols]


def prepare(lanes, lane, barred, kv_blocks):
    rows, width = kv_blocks[0].shape[1:]
    heads, total = width // HEAD_DIM, lanes * rows + CHUNK - ALIGN
    outs = [
        jax.ShapeDtypeStruct((heads, 2 * HEAD_DIM, total), BF16),
        jax.ShapeDtypeStruct((heads, total, 2 * HEAD_DIM), BF16),
    ]
    return pl.pallas_call(
        functools.partial(prepare_kernel, lanes),
        grid=(1,),
        out_shape=outs,
        in_specs=[SMEM, whole(barred)] + [whole(block) for block in kv_blocks],
        out_specs=[whole(out) for out in outs],
        compiler_params=PARAMS,
        cost_estimate=cost(4),
        name="prepare",
    )(lane, barred, *kv_blocks)


def attend_kernel(lanes, shifts, info_ref, hot_ref, text_ref, key_ref, value_ref, *refs):
    count = len(shifts)
    q_refs, out_refs = refs[:count], refs[count : 2 * count]
    q_all, out_all, text_key, text_value = refs[2 * count :]
    rows, width = q_refs[0].shape[1:]
    heads = width // HEAD_DIM
    exponent_scale = math.log2(math.e) / math.sqrt(HEAD_DIM)
    for index in range(count):
        q_all[index] = q_refs[index][0]
    for head in range(heads):
        cols = pl.ds(head * HEAD_DIM, HEAD_DIM)
        text_key[head, :HEAD_DIM] = text_ref[:, cols].astype(F32).T.astype(BF16)
        text_key[head, HEAD_DIM:] = text_ref[:, 2 * width :].astype(F32).T.astype(BF16)
        text_value[head, :, :HEAD_DIM] = text_ref[:, pl.ds(width + head * HEAD_DIM, HEAD_DIM)]
        text_value[head, :, HEAD_DIM:] = jnp.ones_like(text_value[head, :, HEAD_DIM:])

    def block(index, carry):
        shift = info_ref[1 + 2 * lanes + index]
        source = lax.rem(info_ref[0] + lanes - shift, lanes)
        hot = hot_ref[pl.ds(pl.multiple_of(source * rows, rows), rows), :]
        queries = [
            jnp.concatenate([q_all[index, :, head * HEAD_DIM : (head + 1) * HEAD_DIM], hot], axis=1)
            for head in range(heads)
        ]

        def extend(keys, values, state):
            scores = [jnp.dot(queries[h], keys[h], preferred_element_type=F32) for h in range(heads)]
            bounds = [
                jnp.maximum(state[h][0], jnp.max(scores[h], axis=1, keepdims=True)) for h in range(heads)
            ]
            weights = [
                jnp.exp2((scores[h] - bounds[h]) * exponent_scale).astype(BF16) for h in range(heads)
            ]
            shrinks = [jnp.exp2((state[h][0] - bounds[h]) * exponent_scale) for h in range(heads)]
            return [
                (bounds[h], state[h][1] * shrinks[h] + jnp.dot(weights[h], values[h], preferred_element_type=F32))
                for h in range(heads)
            ]

        largest = jnp.full((rows, 1), -1e30, F32)
        total = jnp.zeros((rows, 2 * HEAD_DIM), F32)
        state = extend(
            [text_key[h] for h in range(heads)], [text_value[h] for h in range(heads)], [(largest, total)] * heads
        )
        first = info_ref[1 + source]

        def chunk(number, state):
            place = pl.ds(pl.multiple_of(first + number * CHUNK, ALIGN), CHUNK)
            return extend(
                [key_ref[h, :, place] for h in range(heads)], [value_ref[h, place, :] for h in range(heads)], state
            )

        state = lax.fori_loop(0, info_ref[1 + lanes + source], chunk, state)
        for head in range(heads):
            total = state[head][1]
            result = total[:, :HEAD_DIM] / total[:, HEAD_DIM:]
            out_all[index, :, head * HEAD_DIM : (head + 1) * HEAD_DIM] = result.astype(BF16)
        return carry

    lax.fori_loop(0, count, block, 0)
    for index in range(count):
        out_refs[index][...] = out_all[index]


def attend(lanes, shifts, info, hot, text, keys, values, queries):
    rows, width = queries[0].shape[1:]
    heads, count = width // HEAD_DIM, len(shifts)
    info = jnp.concatenate([info, jnp.array(shifts, jnp.int32)])
    out = jax.ShapeDtypeStruct((rows, width), BF16)
    return pl.pallas_call(
        functools.partial(attend_kernel, lanes, shifts),
        grid=(1,),
        out_shape=[out] * count,
        in_specs=[SMEM] + [whole(a) for a in (hot, text, keys, values, *queries)],
        out_specs=[whole(out)] * count,
        scratch_shapes=[
            pltpu.VMEM((count, rows, width), BF16),
            pltpu.VMEM((count, rows, width), BF16),
            pltpu.VMEM((heads, 2 * HEAD_DIM, text.shape[0]), BF16),
            pltpu.VMEM((heads, text.shape[0], 2 * HEAD_DIM), BF16),
        ],
        compiler_params=PARAMS,
        cost_estimate=cost(1 + 3 * count),
        name="attend",
    )(info, hot, text, keys, values, *queries)


def project_kernel(lanes, lane_ref, weight_ref, gate_ref, *refs):
    blocks, out_ref = refs[:lanes], refs[lanes]
    depth = blocks[0].shape[1]
    total = jnp.zeros(out_ref.shape, F32)
    for shift in range(lanes):
        owner = lax.rem(lane_ref[0] + shift, lanes)
        part = weight_ref[pl.ds(pl.multiple_of(owner * depth, depth), depth), :]
        total += jnp.dot(blocks[shift][...], part, preferred_element_type=F32)
    out_ref[...] = (gate_ref[...] * total).astype(BF16)


def project(lanes, lane, weight, gate_rows, blocks):
    rows, width = gate_rows.shape
    depth, tile = weight.shape[0], width // 3
    return pl.pallas_call(
        functools.partial(project_kernel, lanes),
        grid=(3,),
        out_shape=jax.ShapeDtypeStruct((rows, width), BF16),
        in_specs=[
            SMEM,
            pl.BlockSpec((depth, tile), lambda i: (0, i)),
            pl.BlockSpec((rows, tile), lambda i: (0, i)),
        ]
        + [pl.BlockSpec(blocks[0].shape, lambda i: (0, 0))] * lanes,
        out_specs=pl.BlockSpec((rows, tile), lambda i: (0, i)),
        compiler_params=PARAMS,
        cost_estimate=cost(5),
        name="project",
    )(lane, weight, gate_rows, *blocks)


def on_device(
    t5_attn,
    t5_out_w,
    t5_resid,
    text_dest,
    text_sample,
    kv_weight,
    img_query,
    img_key,
    img_value,
    img_sample,
    proj_weight,
    gate,
):
    groups, lanes = lax.axis_size("dp"), lax.axis_size("seq")
    group, lane = lax.axis_index("dp"), lax.axis_index("seq")
    lane_ref = lane.reshape(1)
    text_count, inner = t5_attn.shape[1:]
    capacity = 2 * text_count // groups
    rows = img_query.shape[1]
    samples = gate.shape[1]

    def shifted(block, shift):
        return lax.ppermute(block, "seq", [(i, (i + shift) % lanes) for i in range(lanes)])

    t5_all = lax.all_gather(jnp.concatenate([t5_attn[0], t5_resid[0]], axis=1), "seq")
    share = inner // groups
    own_w = lax.dynamic_slice_in_dim(t5_out_w, group * share, share, 0)
    both = jnp.concatenate([own_w, proj_weight], axis=1)
    shared = {0: both}
    for step in range(1, lanes // 2 + 1):
        shared[step] = shifted(shared[step - 1], 1)
        if step < lanes // 2:
            shared[lanes - step] = shifted(shared[(lanes - step + 1) % lanes], -1)
    w_rows = jnp.concatenate([shared[s][:, : own_w.shape[1]] for s in range(lanes)], axis=0)
    turned = [shared[s % lanes][:, own_w.shape[1] :] for s in range(lanes, -lanes, -1)]
    turned = jnp.concatenate(turned, axis=0)
    proj_count = proj_weight.shape[0]
    proj_rows = lax.dynamic_slice_in_dim(
        turned, (lanes - lane) * proj_count, lanes * proj_count, 0
    )
    kv_flat = kv_weight.reshape(kv_weight.shape[0], -1)
    own_map = jnp.dot(w_rows, kv_flat, preferred_element_type=F32).astype(BF16)
    map_all = lax.all_to_all(jnp.broadcast_to(own_map[None], (groups,) + own_map.shape), "dp", 0, 0)
    map_all = map_all.reshape(groups, lanes, share, -1).transpose(1, 0, 2, 3).reshape(lanes * inner, -1)
    projection = lax.all_gather(proj_rows, "dp", axis=0, tiled=True)

    target = text_dest[0, :, 0]
    order = jnp.arange(text_count, dtype=jnp.int32)
    ahead = (target[None, :] == target[:, None]) & (order[:, None] < order[None, :])
    slot_of = target * capacity + jnp.sum(ahead.astype(jnp.int32), axis=0)

    sample = img_sample[0]
    column = jnp.arange(HEAD_DIM, dtype=jnp.int32)[None, :]
    hot = (sample[:, None] == column).astype(BF16)
    barred = jnp.where((column < samples) & (sample[:, None] != column), -PENALTY, 0.0).astype(BF16)
    ends = sample.reshape(lanes, rows)
    low = jnp.sum((sample[None, :] < ends[:, :1]).astype(jnp.int32), axis=1) // ALIGN * ALIGN
    high = jnp.sum((sample[None, :] <= ends[:, -1:]).astype(jnp.int32), axis=1)
    info = jnp.concatenate([lane_ref, low, (high - low + CHUNK - 1) // CHUNK]).astype(jnp.int32)

    kv_out = pack(lanes, lane_ref, img_key[0], img_value[0])
    q_out = pack(lanes, lane_ref, img_query[0])
    kv_in, q_in = {0: kv_out[0]}, {0: q_out[0]}
    for shift in ORDER[:3]:
        kv_in[shift] = shifted(kv_out[shift], shift)
    kv_out, _ = lax.optimization_barrier((kv_out, [shared[3], shared[5]]))
    for shift in ORDER[3:]:
        kv_in[shift] = shifted(kv_out[shift], shift)
    q_out, _ = lax.optimization_barrier((q_out, [kv_in[s] for s in ORDER[:4]]))
    for shift in ORDER:
        q_in[shift] = shifted(q_out[shift], shift)

    sent = text_rows(lane_ref, t5_all, map_all, kv_flat, slot_of[None], text_sample, groups * capacity)
    text = lax.all_to_all(sent.reshape(groups, capacity, -1), "dp", 0, 0).reshape(sent.shape)

    keys, values = prepare(lanes, lane_ref, barred, [kv_in[s] for s in range(lanes)])
    returned = {}
    for shifts in SHIFT_GROUPS:
        results = attend(lanes, shifts, info, hot, text, keys, values, [q_in[s] for s in shifts])
        for shift, result in zip(shifts, results):
            returned[shift] = shifted(result, -shift) if shift else result

    own_sample = lax.dynamic_slice_in_dim(sample, lane * rows, rows)
    gate_rows = jnp.zeros((rows, gate.shape[2]), F32)
    for number in range(samples):
        gate_rows = jnp.where(own_sample[:, None] == number, gate[0, number][None, :], gate_rows)
    out = project(lanes, lane_ref, projection, gate_rows, [returned[s] for s in range(lanes)])
    return out[None]


ORDER = (4, 3, 5, 2, 6, 1, 7)
SHIFT_GROUPS = ((4, 3, 5), (2, 6, 1, 7), (0,))


def solution(mesh):
    placed = (
        P("dp", None, "seq"),
        P("seq", None),
        P("dp", None, "seq"),
        P("dp", None, None),
        P("dp", None),
        P(None, None, "seq"),
        P("dp", "seq", None),
        P("dp", "seq", None),
        P("dp", "seq", None),
        P("dp", None),
        P(("dp", "seq"), None),
        P("dp", None, None),
    )
    return jax.shard_map(
        on_device, mesh=mesh, in_specs=placed, out_specs=P("dp", "seq", None), check_vma=False
    )
```

time: 357 us -> 209 us (0.59)
  Pallas kernels: 143 us -> 53.4 us
  blocking collectives: 35.6 us -> 0 us
  local copies, waits for them, and re-layouts: 36.2 us -> 13.6 us
  waiting for transfers between devices: 59.1 us -> 37.7 us
  starting transfers between devices: 59.9 us -> 77 us
    pallas_call x4 -> x7, Pallas kernels: 138 us -> 47.3 us  [the longest x3 29.2 us: attend(): pl.pallas_call(functools.partial(attend_kernel, lanes, shifts), grid=(1,)...]
    all_to_all x1 -> x0, blocking collectives: 35.6 us -> none  [on_device(): lax.all_to_all(jnp.broadcast_to(both[None], (lanes,) + both.shape), 'seq'...]
    ppermute x21 -> x28, waiting for transfers between devices: 59.1 us -> 37.7 us  [shifted(): lax.ppermute(block, 'seq', [(i, (i + shift) % lanes) for i in range(lanes)])]
    unnamed x78 -> x92, local copies, waits for them, and re-layouts: 30.1 us -> 9.45 us
    ppermute x21 -> x28, starting transfers between devices: 45 us -> 61.5 us  [shifted(): lax.ppermute(block, 'seq', [(i, (i + shift) % lanes) for i in range(lanes)])]
  transfers between devices with their start and end apart: 25 -> 32, of which waited for: 10 -> 8; matrix products, arithmetic and copies ran while one was open for 5% -> 10% of each run, Pallas kernels for 39% -> 23%
where the time goes in v2:
time: 209 us; the launch traced here: 207 us
  starting transfers between devices  77 us (37%)
  Pallas kernels  53.4 us (26%)
  waiting for transfers between devices  37.7 us (18%)
  between operations  13.9 us (7%)
  local copies, waits for them, and re-layouts  13.6 us (7%)
  other arithmetic  8.79 us (4%)
  matrix products  3.02 us (1%)
    ppermute x28, starting transfers between devices, shifted(): lax.ppermute(block, 'seq', [(i, (i + shift) % lanes) for i in range(lanes)])  61.5 us
    ppermute x28, waiting for transfers between devices, shifted(): lax.ppermute(block, 'seq', [(i, (i + shift) % lanes) for i in range(lanes)])  37.7 us
    pallas_call x3, Pallas kernels, attend(): pl.pallas_call(functools.partial(attend_kernel, lanes, shifts), grid=(1,)...  29.2 us
    unnamed x92, local copies, waits for them, and re-layouts  9.45 us
    all_to_all x1, starting transfers between devices, on_device(): lax.all_to_all(sent.reshape(groups, capacity, -1), 'dp', 0, 0)  7.96 us
    pallas_call x1, Pallas kernels, text_rows(): pl.pallas_call(functools.partial(text_kernel, steps), grid_spec=pltpu.Pre...  7.59 us
    all_to_all x1, starting transfers between devices, on_device(): lax.all_to_all(jnp.broadcast_to(own_map[None], (groups,) + own_map.shape)...  7.51 us
    pallas_call x1, Pallas kernels, project(): pl.pallas_call(functools.partial(project_kernel, lanes), grid=(3,), out_s...  6.03 us
  transfers between devices with their start and end apart: 32, of which 8 were waited for; matrix products, arithmetic and copies ran while one was open for 10% of the time, Pallas kernels for 23%

profile of v2, /device:TPU:20, one launch (start us, length us, event | category | flops | bytes accessed | tf_op | source)
XLA Modules:
  0.0 207.4 jit_solution(15921535641333281781)
XLA Ops:
  10.1 4.0 %collective-permute-start = (bf16[8,5632]{1,0:T(8,128)(2,1)S(1)}, bf16[8,5632]{1,0:T(8,128)(2,1)S(1)}, u32[]{:S(2)}, u32[]{:S(2)}) collective-permute-start(bf16[8,5632]{1,0:T(8,128)(2,1)S(1)} %pad_maximum_fusion.1), channel_id=1, source_target_pairs={{0,7},{1,0},{2,1},{3,2},{4,3},{5,4},{6,5},{7,6},{8,15},{9,8},{10,9... | collective-permute-start | bytes 270344 | tf_op jit(solution)/shard_map/ppermute | solution.py:301
  14.1 3.2 %pack.2 = (bf16[2,256,256]{2,1,0:T(8,128)(2,1)}, bf16[2,256,256]{2,1,0:T(8,128)(2,1)}, bf16[2,256,256]{2,1,0:T(8,128)(2,1)}, bf16[2,256,256]{2,1,0:T(8,128)(2,1)...) custom-call(s32[1]{0:T(128)} %bitcast.lane_ref, ...), custom_call_target="tpu_custom_call" | custom-call | flops 2200000000 | tf_op jit(solution)/shard_map/pack/pallas_call | solution.py:45
  17.3 4.5 %collective-permute-start.10 = (bf16[2,256,256]{2,1,0:T(8,128)(2,1)}, bf16[2,256,256]{2,1,0:T(8,128)(2,1)S(1)}, u32[]{:S(2)}, u32[]{:S(2)}) collective-permute-start(bf16[2,256,256]{2,1,0:T(8,128)(2,1)} %get-tuple-element.45), channel_id=1, source_target_pairs={{0,4},{1,5},{2,6},{3,7},{4,0},{5,1},{6,2},{7,3},{8,12},{9,13},{10,... | collective-permute-start | bytes 786440 | tf_op jit(solution)/shard_map/ppermute | solution.py:301
  21.8 3.8 %collective-permute-start.9 = (bf16[2,256,256]{2,1,0:T(8,128)(2,1)}, bf16[2,256,256]{2,1,0:T(8,128)(2,1)S(1)}, u32[]{:S(2)}, u32[]{:S(2)}) collective-permute-start(bf16[2,256,256]{2,1,0:T(8,128)(2,1)} %get-tuple-element.44), channel_id=1, source_target_pairs={{0,3},{1,4},{2,5},{3,6},{4,7},{5,0},{6,1},{7,2},{8,11},{9,12},{10,... | collective-permute-start | bytes 786440 | tf_op jit(solution)/shard_map/ppermute | solution.py:301
  26.4 5.0 %copy.26 = bf16[512,8,2,256]{3,1,2,0:T(8,128)(2,1)} copy(bf16[512,8,2,256]{3,2,1,0:T(2,128)(2,1)} %bitcast.29) | data formatting | bytes 8388608
  37.2 18.1 %collective-permute-done.4 = bf16[8,5632]{1,0:T(8,128)(2,1)S(1)} collective-permute-done((bf16[8,5632]{1,0:T(8,128)(2,1)S(1)}, bf16[8,5632]{1,0:T(8,128)(2,1)S(1)}, u32[]{:S(2)}, u32[]{:S(2)}) %collective-permute-start.4) | collective-permute-done | bytes 90144 | tf_op jit(solution)/shard_map/ppermute | solution.py:301
  58.0 2.7 %collective-permute-start.2 = (bf16[8,5632]{1,0:T(8,128)(2,1)S(1)}, bf16[8,5632]{1,0:T(8,128)(2,1)S(1)}, u32[]{:S(2)}, u32[]{:S(2)}) collective-permute-start(bf16[8,5632]{1,0:T(8,128)(2,1)S(1)} %collective-permute-done.1), channel_id=1, source_target_pairs={{0,7},{1,0},{2,1},{3,2},{4,3},{5,4},{6,5},{7,6},{8,15},{9,8},{10,9... | collective-permute-start | bytes 270344 | tf_op jit(solution)/shard_map/ppermute | solution.py:301
  64.4 5.7 %collective-permute-done.6 = bf16[8,5632]{1,0:T(8,128)(2,1)S(1)} collective-permute-done((bf16[8,5632]{1,0:T(8,128)(2,1)S(1)}, bf16[8,5632]{1,0:T(8,128)(2,1)S(1)}, u32[]{:S(2)}, u32[]{:S(2)}) %collective-permute-start.6) | collective-permute-done | bytes 90144 | tf_op jit(solution)/shard_map/ppermute | solution.py:301
  71.0 3.0 %convolution_convert_fusion = bf16[64,512]{1,0:T(8,128)(2,1)S(1)} fusion(bf16[64,4096]{1,0:T(8,128)(2,1)S(1)} %slice_dynamic-update-slice_fusion, bf16[4096,512]{1,0:T(8,128)(2,1)} %bitcast.26), kind=kOutput, calls=%fused_computation.1 | convolution fusion | flops 268468224 | bytes 4784128 | tf_op jit(solution)/shard_map/dot_general | solution.py:320
  75.7 7.5 %all-to-all-start = ((bf16[32,64,512]{2,1,0:T(8,128)(2,1)}), bf16[32,64,512]{2,1,0:T(8,128)(2,1)S(1)}, u32[]{:S(2)}, u32[]{:S(2)}) async-start(bf16[32,64,512]{2,1,0:T(8,128)(2,1)} %broadcast_in_dim.95), calls=%async_computation | async-start | bytes 4194304 | tf_op jit(solution)/shard_map/all_to_all | solution.py:321
  92.4 3.0 %collective-permute-start.12 = (bf16[2,256,256]{2,1,0:T(8,128)(2,1)}, bf16[2,256,256]{2,1,0:T(8,128)(2,1)}, u32[]{:S(2)}, u32[]{:S(2)}) collective-permute-start(bf16[2,256,256]{2,1,0:T(8,128)(2,1)} %get-tuple-element.51), channel_id=1, source_target_pairs={{0,6},{1,7},{2,0},{3,1},{4,2},{5,3},{6,4},{7,5},{8,14},{9,15},{10,... | collective-permute-start | bytes 786440 | tf_op jit(solution)/shard_map/ppermute | solution.py:301
  97.7 9.2 %collective-permute-done.8.refs_2_ = bf16[2,256,256]{2,1,0:T(8,128)(2,1)S(1)} collective-permute-done((bf16[2,256,256]{2,1,0:T(8,128)(2,1)S(1)}, bf16[2,256,256]{2,1,0:T(8,128)(2,1)S(1)}, u32[]{:S(2)}, u32[]{:S(2)}) %collective-permute-start.8) | collective-permute-done | bytes 262176 | tf_op jit(solution)/shard_map/ppermute | solution.py:301
  106.9 4.4 %collective-permute-start.20 = (bf16[1,256,256]{2,1,0:T(8,128)(2,1)}, bf16[1,256,256]{2,1,0:T(8,128)(2,1)}, u32[]{:S(2)}, u32[]{:S(2)}) collective-permute-start(bf16[1,256,256]{2,1,0:T(8,128)(2,1)} %get-tuple-element.69), channel_id=1, source_target_pairs={{0,4},{1,5},{2,6},{3,7},{4,0},{5,1},{6,2},{7,3},{8,12},{9,13},{10,... | collective-permute-start | bytes 393224 | tf_op jit(solution)/shard_map/ppermute | solution.py:301
  112.9 7.6 %text_rows.1 = bf16[256,640]{1,0:T(8,128)(2,1)} custom-call(s32[1]{0:T(128)} %bitcast.lane_ref, bf16[8,128,768]{2,1,0:T(8,128)(2,1)} %bitcast.42, bf16[2048,512]{1,0:T(8,128)(2,1)} %bitcast.30, bf16[4096,512]{1,0:T(8,128)(2,1)} %bitcast.27, s32[1,128]{1,0:T(1,128)} %bitcast_add_fusion.slot_ref, s32[1,128]{1,0:T(1,128)} %sample_ref.1), custom_call_target="tpu_custom_call" | custom-call | flops 5500000256 | tf_op jit(solution)/shard_map/text_rows/pallas_call | solution.py:97
  120.5 8.0 %all-to-all-start.1 = ((bf16[32,8,640]{2,1,0:T(8,128)(2,1)}), bf16[32,8,640]{2,1,0:T(8,128)(2,1)S(1)}, u32[]{:S(2)}, u32[]{:S(2)}) async-start(bf16[32,8,640]{2,1,0:T(8,128)(2,1)} %bitcast.34), calls=%async_computation.1 | async-start | bytes 655360 | tf_op jit(solution)/shard_map/all_to_all | solution.py:352
  128.5 4.8 %collective-permute-start.22 = (bf16[1,256,256]{2,1,0:T(8,128)(2,1)S(1)}, bf16[1,256,256]{2,1,0:T(8,128)(2,1)S(1)}, u32[]{:S(2)}, u32[]{:S(2)}) collective-permute-start(bf16[1,256,256]{2,1,0:T(8,128)(2,1)S(1)} %copy-done.19), channel_id=1, source_target_pairs={{0,5},{1,6},{2,7},{3,0},{4,1},{5,2},{6,3},{7,4},{8,13},{9,14},{10,... | collective-permute-start | bytes 393224 | tf_op jit(solution)/shard_map/ppermute | solution.py:301
  133.4 4.1 %collective-permute-start.15 = (bf16[1,256,256]{2,1,0:T(8,128)(2,1)S(1)}, bf16[1,256,256]{2,1,0:T(8,128)(2,1)S(1)}, u32[]{:S(2)}, u32[]{:S(2)}) collective-permute-start(bf16[1,256,256]{2,1,0:T(8,128)(2,1)S(1)} %copy-done.17), channel_id=1, source_target_pairs={{0,6},{1,7},{2,0},{3,1},{4,2},{5,3},{6,4},{7,5},{8,14},{9,15},{10,... | collective-permute-start | bytes 393224 | tf_op jit(solution)/shard_map/ppermute | solution.py:301
  137.5 5.0 %prepare.1 = (bf16[2,256,2816]{2,1,0:T(8,128)(2,1)}, bf16[2,2816,256]{2,1,0:T(8,128)(2,1)}) custom-call(s32[1]{0:T(128)} %bitcast.lane_ref, bf16[2048,128]{1,0:T(8,128)(2,1)} %select_convert_fusion.bar_ref, bf16[2,256,256]{2,1,0:T(8,128)(2,1)} %get-tuple-element.41.refs_0_, bf16[2,256,256]{2,1,0:T(8,128)(2,1)} %collective-permute-done.7.refs_1_, ...), custom_call_target="tpu_custom_call" | custom-call | flops 4400000000 | tf_op jit(solution)/shard_map/prepare/pallas_call | solution.py:148
  146.6 11.6 %attend.5 = (bf16[256,256]{1,0:T(8,128)(2,1)}, bf16[256,256]{1,0:T(8,128)(2,1)}, bf16[256,256]{1,0:T(8,128)(2,1)}) custom-call(s32[20]{0:T(128)} %pad_add_fusion.2.info_ref, bf16[2048,128]{1,0:T(8,128)(2,1)} %fusion.hot_ref, bf16[256,640]{1,0:T(8,128)(2,1)} %bitcast.31, bf16[2,256,2816]{2,1,0:T(8,128)(2,1)} %get-tuple-element.53.key_ref, ...), custom_call_target="tpu_custom_call" | custom-call | flops 11000000512 | tf_op jit(solution)/shard_map/attend/pallas_call | solution.py:229
  160.1 3.1 %collective-permute-start.24 = (bf16[256,256]{1,0:T(8,128)(2,1)}, bf16[256,256]{1,0:T(8,128)(2,1)S(1)}, u32[]{:S(2)}, u32[]{:S(2)}) collective-permute-start(bf16[256,256]{1,0:T(8,128)(2,1)} %get-tuple-element.73), channel_id=1, source_target_pairs={{0,4},{1,5},{2,6},{3,7},{4,0},{5,1},{6,2},{7,3},{8,12},{9,13},{10,... | collective-permute-start | bytes 393224 | tf_op jit(solution)/shard_map/ppermute | solution.py:301
  164.5 12.3 %attend.4 = (bf16[256,256]{1,0:T(8,128)(2,1)}, bf16[256,256]{1,0:T(8,128)(2,1)}, bf16[256,256]{1,0:T(8,128)(2,1)}, bf16[256,256]{1,0:T(8,128)(2,1)}) custom-call(s32[21]{0:T(128)} %pad_add_fusion.1.info_ref, bf16[2048,128]{1,0:T(8,128)(2,1)} %fusion.hot_ref, bf16[256,640]{1,0:T(8,128)(2,1)} %bitcast.32, bf16[2,256,2816]{2,1,0:T(8,128)(2,1)} %get-tuple-element.53.key_ref, ...), custom_call_target="tpu_custom_call" | custom-call | flops 14300000256 | tf_op jit(solution)/shard_map/attend/pallas_call | solution.py:229
  178.4 5.9 %collective-permute-start.19 = (bf16[256,256]{1,0:T(8,128)(2,1)}, bf16[256,256]{1,0:T(8,128)(2,1)S(1)}, u32[]{:S(2)}, u32[]{:S(2)}) collective-permute-start(bf16[256,256]{1,0:T(8,128)(2,1)} %get-tuple-element.68), channel_id=1, source_target_pairs={{0,6},{1,7},{2,0},{3,1},{4,2},{5,3},{6,4},{7,5},{8,14},{9,15},{10,... | collective-permute-start | bytes 393224 | tf_op jit(solution)/shard_map/ppermute | solution.py:301
  185.3 5.3 %attend.3.refs_0_ = bf16[256,256]{1,0:T(8,128)(2,1)} custom-call(s32[18]{0:T(128)} %pad_add_fusion.info_ref, bf16[2048,128]{1,0:T(8,128)(2,1)} %fusion.hot_ref, bf16[256,640]{1,0:T(8,128)(2,1)} %bitcast.33, bf16[2,256,2816]{2,1,0:T(8,128)(2,1)} %get-tuple-element.53.key_ref, bf16[2,2816,256]{2,1,0:T(8,128)(2,1)} %get-tuple-element.54.value_ref, ...), custom_call_target="tpu_custom_call" | custom-call | flops 4400000000 | tf_op jit(solution)/shard_map/attend/pallas_call | solution.py:229
  194.5 6.0 %project.1 = bf16[256,1536]{1,0:T(8,128)(2,1)} custom-call(s32[1]{0:T(128)} %bitcast.lane_ref, bf16[2048,1536]{1,0:T(8,128)(2,1)} %all-gather.4.cloned.1.call-done.weight_ref, f32[256,1536]{1,0:T(8,128)} %select_select_fusion.gate_ref, bf16[256,256]{1,0:T(8,128)(2,1)} %attend.3.refs_0_, bf16[256,256]{1,0:T(8,128)(2,1)} %copy-done.27, ...), custom_call_target="tpu_custom_call" | custom-call | flops 5500000256 | tf_op jit(solution)/shard_map/project/pallas_call | solution.py:261
  (166 shorter events, 45.6 us)
Async XLA Ops:
  6.5 106.4 %all-gather.6.cloned.1.call-start = ((), (), s32[]{:S(2)}) async-start(), calls=%async_computation.3 | async-start | bytes 1769472 | tf_op jit(solution)/shard_map/all_gather | solution.py:303
  8.1 25.8 %collective-permute-start.3 = (bf16[8,5632]{1,0:T(8,128)(2,1)S(1)}, bf16[8,5632]{1,0:T(8,128)(2,1)S(1)}, u32[]{:S(2)}, u32[]{:S(2)}) collective-permute-start(bf16[8,5632]{1,0:T(8,128)(2,1)S(1)} %pad_maximum_fusion.1), channel_id=1, source_target_pairs={{0,1},{1,2},{2,3},{3,4},{4,5},{5,6},{6,7},{7,0},{8,9},{9,10},{10,1... | collective-permute-start | bytes 270344 | tf_op jit(solution)/shard_map/ppermute | solution.py:301
  10.1 24.9 %collective-permute-start = (bf16[8,5632]{1,0:T(8,128)(2,1)S(1)}, bf16[8,5632]{1,0:T(8,128)(2,1)S(1)}, u32[]{:S(2)}, u32[]{:S(2)}) collective-permute-start(bf16[8,5632]{1,0:T(8,128)(2,1)S(1)} %pad_maximum_fusion.1), channel_id=1, source_target_pairs={{0,7},{1,0},{2,1},{3,2},{4,3},{5,4},{6,5},{7,6},{8,15},{9,8},{10,9... | collective-permute-start | bytes 270344 | tf_op jit(solution)/shard_map/ppermute | solution.py:301
  17.3 78.2 %collective-permute-start.10 = (bf16[2,256,256]{2,1,0:T(8,128)(2,1)}, bf16[2,256,256]{2,1,0:T(8,128)(2,1)S(1)}, u32[]{:S(2)}, u32[]{:S(2)}) collective-permute-start(bf16[2,256,256]{2,1,0:T(8,128)(2,1)} %get-tuple-element.45), channel_id=1, source_target_pairs={{0,4},{1,5},{2,6},{3,7},{4,0},{5,1},{6,2},{7,3},{8,12},{9,13},{10,... | collective-permute-start | bytes 786440 | tf_op jit(solution)/shard_map/ppermute | solution.py:301
  21.7 75.0 %collective-permute-start.11 = (bf16[2,256,256]{2,1,0:T(8,128)(2,1)}, bf16[2,256,256]{2,1,0:T(8,128)(2,1)S(1)}, u32[]{:S(2)}, u32[]{:S(2)}) collective-permute-start(bf16[2,256,256]{2,1,0:T(8,128)(2,1)} %get-tuple-element.46), channel_id=1, source_target_pairs={{0,5},{1,6},{2,7},{3,0},{4,1},{5,2},{6,3},{7,4},{8,13},{9,14},{10,... | collective-permute-start | bytes 786440 | tf_op jit(solution)/shard_map/ppermute | solution.py:301
  21.8 75.9 %collective-permute-start.9 = (bf16[2,256,256]{2,1,0:T(8,128)(2,1)}, bf16[2,256,256]{2,1,0:T(8,128)(2,1)S(1)}, u32[]{:S(2)}, u32[]{:S(2)}) collective-permute-start(bf16[2,256,256]{2,1,0:T(8,128)(2,1)} %get-tuple-element.44), channel_id=1, source_target_pairs={{0,3},{1,4},{2,5},{3,6},{4,7},{5,0},{6,1},{7,2},{8,11},{9,12},{10,... | collective-permute-start | bytes 786440 | tf_op jit(solution)/shard_map/ppermute | solution.py:301
  26.3 167.5 %all-gather.4.cloned.1.call-start = ((), (), s32[]{:S(2)}) async-start(), calls=%async_computation.2 | async-start | bytes 6488064 | tf_op jit(solution)/shard_map/all_gather | solution.py:323
  33.9 21.3 %collective-permute-start.4 = (bf16[8,5632]{1,0:T(8,128)(2,1)S(1)}, bf16[8,5632]{1,0:T(8,128)(2,1)S(1)}, u32[]{:S(2)}, u32[]{:S(2)}) collective-permute-start(bf16[8,5632]{1,0:T(8,128)(2,1)S(1)} %collective-permute-done.3), channel_id=1, source_target_pairs={{0,1},{1,2},{2,3},{3,4},{4,5},{5,6},{6,7},{7,0},{8,9},{9,10},{10,1... | collective-permute-start | bytes 270344 | tf_op jit(solution)/shard_map/ppermute | solution.py:301
  35.0 23.0 %collective-permute-start.1 = (bf16[8,5632]{1,0:T(8,128)(2,1)S(1)}, bf16[8,5632]{1,0:T(8,128)(2,1)S(1)}, u32[]{:S(2)}, u32[]{:S(2)}) collective-permute-start(bf16[8,5632]{1,0:T(8,128)(2,1)S(1)} %collective-permute-done), channel_id=1, source_target_pairs={{0,7},{1,0},{2,1},{3,2},{4,3},{5,4},{6,5},{7,6},{8,15},{9,8},{10,9... | collective-permute-start | bytes 270344 | tf_op jit(solution)/shard_map/ppermute | solution.py:301
  75.7 35.5 %all-to-all-start = ((bf16[32,64,512]{2,1,0:T(8,128)(2,1)}), bf16[32,64,512]{2,1,0:T(8,128)(2,1)S(1)}, u32[]{:S(2)}, u32[]{:S(2)}) async-start(bf16[32,64,512]{2,1,0:T(8,128)(2,1)} %broadcast_in_dim.95), calls=%async_computation | async-start | bytes 4194304 | tf_op jit(solution)/shard_map/all_to_all | solution.py:321
  92.4 36.1 %collective-permute-start.12 = (bf16[2,256,256]{2,1,0:T(8,128)(2,1)}, bf16[2,256,256]{2,1,0:T(8,128)(2,1)}, u32[]{:S(2)}, u32[]{:S(2)}) collective-permute-start(bf16[2,256,256]{2,1,0:T(8,128)(2,1)} %get-tuple-element.51), channel_id=1, source_target_pairs={{0,6},{1,7},{2,0},{3,1},{4,2},{5,3},{6,4},{7,5},{8,14},{9,15},{10,... | collective-permute-start | bytes 786440 | tf_op jit(solution)/shard_map/ppermute | solution.py:301
  95.5 37.9 %collective-permute-start.13 = (bf16[2,256,256]{2,1,0:T(8,128)(2,1)S(1)}, bf16[2,256,256]{2,1,0:T(8,128)(2,1)}, u32[]{:S(2)}, u32[]{:S(2)}) collective-permute-start(bf16[2,256,256]{2,1,0:T(8,128)(2,1)S(1)} %copy-done.12), channel_id=1, source_target_pairs={{0,7},{1,0},{2,1},{3,2},{4,3},{5,4},{6,5},{7,6},{8,15},{9,8},{10,9... | collective-permute-start | bytes 786440 | tf_op jit(solution)/shard_map/ppermute | solution.py:301
  96.7 36.6 %collective-permute-start.7 = (bf16[2,256,256]{2,1,0:T(8,128)(2,1)S(1)}, bf16[2,256,256]{2,1,0:T(8,128)(2,1)}, u32[]{:S(2)}, u32[]{:S(2)}) collective-permute-start(bf16[2,256,256]{2,1,0:T(8,128)(2,1)S(1)} %copy-done.11), channel_id=1, source_target_pairs={{0,1},{1,2},{2,3},{3,4},{4,5},{5,6},{6,7},{7,0},{8,9},{9,10},{10,1... | collective-permute-start | bytes 786440 | tf_op jit(solution)/shard_map/ppermute | solution.py:301
  106.9 35.7 %collective-permute-start.20 = (bf16[1,256,256]{2,1,0:T(8,128)(2,1)}, bf16[1,256,256]{2,1,0:T(8,128)(2,1)}, u32[]{:S(2)}, u32[]{:S(2)}) collective-permute-start(bf16[1,256,256]{2,1,0:T(8,128)(2,1)} %get-tuple-element.69), channel_id=1, source_target_pairs={{0,4},{1,5},{2,6},{3,7},{4,0},{5,1},{6,2},{7,3},{8,12},{9,13},{10,... | collective-permute-start | bytes 393224 | tf_op jit(solution)/shard_map/ppermute | solution.py:301
  111.3 33.0 %collective-permute-start.21 = (bf16[1,256,256]{2,1,0:T(8,128)(2,1)}, bf16[1,256,256]{2,1,0:T(8,128)(2,1)}, u32[]{:S(2)}, u32[]{:S(2)}) collective-permute-start(bf16[1,256,256]{2,1,0:T(8,128)(2,1)} %get-tuple-element.70), channel_id=1, source_target_pairs={{0,3},{1,4},{2,5},{3,6},{4,7},{5,0},{6,1},{7,2},{8,11},{9,12},{10,... | collective-permute-start | bytes 393224 | tf_op jit(solution)/shard_map/ppermute | solution.py:301
  120.5 25.3 %all-to-all-start.1 = ((bf16[32,8,640]{2,1,0:T(8,128)(2,1)}), bf16[32,8,640]{2,1,0:T(8,128)(2,1)S(1)}, u32[]{:S(2)}, u32[]{:S(2)}) async-start(bf16[32,8,640]{2,1,0:T(8,128)(2,1)} %bitcast.34), calls=%async_computation.1 | async-start | bytes 655360 | tf_op jit(solution)/shard_map/all_to_all | solution.py:352
  128.5 17.3 %collective-permute-start.22 = (bf16[1,256,256]{2,1,0:T(8,128)(2,1)S(1)}, bf16[1,256,256]{2,1,0:T(8,128)(2,1)S(1)}, u32[]{:S(2)}, u32[]{:S(2)}) collective-permute-start(bf16[1,256,256]{2,1,0:T(8,128)(2,1)S(1)} %copy-done.19), channel_id=1, source_target_pairs={{0,5},{1,6},{2,7},{3,0},{4,1},{5,2},{6,3},{7,4},{8,13},{9,14},{10,... | collective-permute-start | bytes 393224 | tf_op jit(solution)/shard_map/ppermute | solution.py:301
  133.4 26.7 %collective-permute-start.14 = (bf16[1,256,256]{2,1,0:T(8,128)(2,1)S(1)}, bf16[1,256,256]{2,1,0:T(8,128)(2,1)S(1)}, u32[]{:S(2)}, u32[]{:S(2)}) collective-permute-start(bf16[1,256,256]{2,1,0:T(8,128)(2,1)S(1)} %copy-done.18), channel_id=1, source_target_pairs={{0,2},{1,3},{2,4},{3,5},{4,6},{5,7},{6,0},{7,1},{8,10},{9,11},{10,... | collective-permute-start | bytes 393224 | tf_op jit(solution)/shard_map/ppermute | solution.py:301
  133.4 29.8 %collective-permute-start.15 = (bf16[1,256,256]{2,1,0:T(8,128)(2,1)S(1)}, bf16[1,256,256]{2,1,0:T(8,128)(2,1)S(1)}, u32[]{:S(2)}, u32[]{:S(2)}) collective-permute-start(bf16[1,256,256]{2,1,0:T(8,128)(2,1)S(1)} %copy-done.17), channel_id=1, source_target_pairs={{0,6},{1,7},{2,0},{3,1},{4,2},{5,3},{6,4},{7,5},{8,14},{9,15},{10,... | collective-permute-start | bytes 393224 | tf_op jit(solution)/shard_map/ppermute | solution.py:301
  142.5 20.6 %collective-permute-start.16 = (bf16[1,256,256]{2,1,0:T(8,128)(2,1)S(1)}, bf16[1,256,256]{2,1,0:T(8,128)(2,1)S(1)}, u32[]{:S(2)}, u32[]{:S(2)}) collective-permute-start(bf16[1,256,256]{2,1,0:T(8,128)(2,1)S(1)} %copy-done.16), channel_id=1, source_target_pairs={{0,1},{1,2},{2,3},{3,4},{4,5},{5,6},{6,7},{7,0},{8,9},{9,10},{10,1... | collective-permute-start | bytes 393224 | tf_op jit(solution)/shard_map/ppermute | solution.py:301
  144.3 18.9 %collective-permute-start.17 = (bf16[1,256,256]{2,1,0:T(8,128)(2,1)S(1)}, bf16[1,256,256]{2,1,0:T(8,128)(2,1)S(1)}, u32[]{:S(2)}, u32[]{:S(2)}) collective-permute-start(bf16[1,256,256]{2,1,0:T(8,128)(2,1)S(1)} %copy-done.15), channel_id=1, source_target_pairs={{0,7},{1,0},{2,1},{3,2},{4,3},{5,4},{6,5},{7,6},{8,15},{9,8},{10,9... | collective-permute-start | bytes 393224 | tf_op jit(solution)/shard_map/ppermute | solution.py:301
  158.2 26.1 %collective-permute-start.23 = (bf16[256,256]{1,0:T(8,128)(2,1)}, bf16[256,256]{1,0:T(8,128)(2,1)S(1)}, u32[]{:S(2)}, u32[]{:S(2)}) collective-permute-start(bf16[256,256]{1,0:T(8,128)(2,1)} %get-tuple-element.72), channel_id=1, source_target_pairs={{0,5},{1,6},{2,7},{3,0},{4,1},{5,2},{6,3},{7,4},{8,13},{9,14},{10,... | collective-permute-start | bytes 393224 | tf_op jit(solution)/shard_map/ppermute | solution.py:301
  160.1 24.3 %collective-permute-start.24 = (bf16[256,256]{1,0:T(8,128)(2,1)}, bf16[256,256]{1,0:T(8,128)(2,1)S(1)}, u32[]{:S(2)}, u32[]{:S(2)}) collective-permute-start(bf16[256,256]{1,0:T(8,128)(2,1)} %get-tuple-element.73), channel_id=1, source_target_pairs={{0,4},{1,5},{2,6},{3,7},{4,0},{5,1},{6,2},{7,3},{8,12},{9,13},{10,... | collective-permute-start | bytes 393224 | tf_op jit(solution)/shard_map/ppermute | solution.py:301
  163.2 27.5 %collective-permute-start.25 = (bf16[256,256]{1,0:T(8,128)(2,1)}, bf16[256,256]{1,0:T(8,128)(2,1)S(1)}, u32[]{:S(2)}, u32[]{:S(2)}) collective-permute-start(bf16[256,256]{1,0:T(8,128)(2,1)} %get-tuple-element.74), channel_id=1, source_target_pairs={{0,3},{1,4},{2,5},{3,6},{4,7},{5,0},{6,1},{7,2},{8,11},{9,12},{10,... | collective-permute-start | bytes 393224 | tf_op jit(solution)/shard_map/ppermute | solution.py:301
  (41 other events, 342.9 us)
Sparse Core Ops, SparseCore 0:
  26.4 47.4 all-gather.5
  76.5 68.1 all-gather.3

commit v3 on v2

--- a/solution.py
+++ b/solution.py
@@ -339,12 +339,12 @@
     kv_out = pack(lanes, lane_ref, img_key[0], img_value[0])
     q_out = pack(lanes, lane_ref, img_query[0])
     kv_in, q_in = {0: kv_out[0]}, {0: q_out[0]}
-    for shift in ORDER[:3]:
+    for shift in NEAR:
         kv_in[shift] = shifted(kv_out[shift], shift)
     kv_out, _ = lax.optimization_barrier((kv_out, [shared[3], shared[5]]))
-    for shift in ORDER[3:]:
+    for shift in FAR:
         kv_in[shift] = shifted(kv_out[shift], shift)
-    q_out, _ = lax.optimization_barrier((q_out, [kv_in[s] for s in ORDER[:4]]))
+    q_out, _ = lax.optimization_barrier((q_out, [kv_in[s] for s in (*NEAR, FAR[0])]))
     for shift in ORDER:
         q_in[shift] = shifted(q_out[shift], shift)
 
@@ -367,6 +367,7 @@
 
 
 ORDER = (4, 3, 5, 2, 6, 1, 7)
+NEAR, FAR = (1, 7, 2), (4, 3, 5, 6)
 SHIFT_GROUPS = ((4, 3, 5), (2, 6, 1, 7), (0,))
 
 

time: 209 us -> 203 us (0.971)
  starting transfers between devices: 77 us -> 63.6 us
  waiting for transfers between devices: 37.7 us -> 45.5 us
    ppermute x28, starting transfers between devices: 61.5 us -> 47.5 us  [shifted(): lax.ppermute(block, 'seq', [(i, (i + shift) % lanes) for i in range(lanes)])]
    ppermute x28, waiting for transfers between devices: 37.7 us -> 45.5 us  [shifted(): lax.ppermute(block, 'seq', [(i, (i + shift) % lanes) for i in range(lanes)])]
  transfers between devices with their start and end apart: 32 -> 32, of which waited for: 8 -> 7; matrix products, arithmetic and copies ran while one was open for 10% -> 10% of each run, Pallas kernels for 23% -> 23%
where the time goes in v3:
time: 203 us; the launch traced here: 202 us
  starting transfers between devices  63.6 us (31%)
  Pallas kernels  53.2 us (26%)
  waiting for transfers between devices  45.5 us (22%)
  between operations  13.9 us (7%)
  local copies, waits for them, and re-layouts  13.5 us (7%)
  other arithmetic  8.79 us (4%)
  matrix products  3.02 us (1%)
    ppermute x28, starting transfers between devices, shifted(): lax.ppermute(block, 'seq', [(i, (i + shift) % lanes) for i in range(lanes)])  47.5 us
    ppermute x28, waiting for transfers between devices, shifted(): lax.ppermute(block, 'seq', [(i, (i + shift) % lanes) for i in range(lanes)])  45.5 us
    pallas_call x3, Pallas kernels, attend(): pl.pallas_call(functools.partial(attend_kernel, lanes, shifts), grid=(1,)...  29.2 us
    unnamed x92, local copies, waits for them, and re-layouts  9.41 us
    all_to_all x1, starting transfers between devices, on_device(): lax.all_to_all(sent.reshape(groups, capacity, -1), 'dp', 0, 0)  8.5 us
    pallas_call x1, Pallas kernels, text_rows(): pl.pallas_call(functools.partial(text_kernel, steps), grid_spec=pltpu.Pre...  7.58 us
    all_to_all x1, starting transfers between devices, on_device(): lax.all_to_all(jnp.broadcast_to(own_map[None], (groups,) + own_map.shape)...  7.51 us
    pallas_call x1, Pallas kernels, project(): pl.pallas_call(functools.partial(project_kernel, lanes), grid=(3,), out_s...  6.03 us
  transfers between devices with their start and end apart: 32, of which 7 were waited for; matrix products, arithmetic and copies ran while one was open for 10% of the time, Pallas kernels for 23%

profile of v3, /device:TPU:20, one launch (start us, length us, event | category | flops | bytes accessed | tf_op | source)
XLA Modules:
  0.0 201.6 jit_solution(7267878692890185124)
XLA Ops:
  10.1 4.0 %collective-permute-start = (bf16[8,5632]{1,0:T(8,128)(2,1)S(1)}, bf16[8,5632]{1,0:T(8,128)(2,1)S(1)}, u32[]{:S(2)}, u32[]{:S(2)}) collective-permute-start(bf16[8,5632]{1,0:T(8,128)(2,1)S(1)} %pad_maximum_fusion.1), channel_id=1, source_target_pairs={{0,7},{1,0},{2,1},{3,2},{4,3},{5,4},{6,5},{7,6},{8,15},{9,8},{10,9... | collective-permute-start | bytes 270344 | tf_op jit(solution)/shard_map/ppermute | solution.py:301
  14.1 3.2 %pack.2 = (bf16[2,256,256]{2,1,0:T(8,128)(2,1)}, bf16[2,256,256]{2,1,0:T(8,128)(2,1)}, bf16[2,256,256]{2,1,0:T(8,128)(2,1)}, bf16[2,256,256]{2,1,0:T(8,128)(2,1)...) custom-call(s32[1]{0:T(128)} %bitcast.lane_ref, ...), custom_call_target="tpu_custom_call" | custom-call | flops 2200000000 | tf_op jit(solution)/shard_map/pack/pallas_call | solution.py:45
  20.5 5.0 %copy.26 = bf16[512,8,2,256]{3,1,2,0:T(8,128)(2,1)} copy(bf16[512,8,2,256]{3,2,1,0:T(2,128)(2,1)} %bitcast.29) | data formatting | bytes 8388608
  28.0 3.2 %collective-permute-start.4 = (bf16[8,5632]{1,0:T(8,128)(2,1)S(1)}, bf16[8,5632]{1,0:T(8,128)(2,1)S(1)}, u32[]{:S(2)}, u32[]{:S(2)}) collective-permute-start(bf16[8,5632]{1,0:T(8,128)(2,1)S(1)} %collective-permute-done.3), channel_id=1, source_target_pairs={{0,1},{1,2},{2,3},{3,4},{4,5},{5,6},{6,7},{7,0},{8,9},{9,10},{10,1... | collective-permute-start | bytes 270344 | tf_op jit(solution)/shard_map/ppermute | solution.py:301
  31.2 15.6 %collective-permute-done.4 = bf16[8,5632]{1,0:T(8,128)(2,1)S(1)} collective-permute-done((bf16[8,5632]{1,0:T(8,128)(2,1)S(1)}, bf16[8,5632]{1,0:T(8,128)(2,1)S(1)}, u32[]{:S(2)}, u32[]{:S(2)}) %collective-permute-start.4) | collective-permute-done | bytes 90144 | tf_op jit(solution)/shard_map/ppermute | solution.py:301
  46.9 3.2 %collective-permute-start.2 = (bf16[8,5632]{1,0:T(8,128)(2,1)S(1)}, bf16[8,5632]{1,0:T(8,128)(2,1)S(1)}, u32[]{:S(2)}, u32[]{:S(2)}) collective-permute-start(bf16[8,5632]{1,0:T(8,128)(2,1)S(1)} %collective-permute-done.1), channel_id=1, source_target_pairs={{0,7},{1,0},{2,1},{3,2},{4,3},{5,4},{6,5},{7,6},{8,15},{9,8},{10,9... | collective-permute-start | bytes 270344 | tf_op jit(solution)/shard_map/ppermute | solution.py:301
  50.1 4.9 %collective-permute-done.5 = bf16[8,5632]{1,0:T(8,128)(2,1)S(1)} collective-permute-done((bf16[8,5632]{1,0:T(8,128)(2,1)S(1)}, bf16[8,5632]{1,0:T(8,128)(2,1)S(1)}, u32[]{:S(2)}, u32[]{:S(2)}) %collective-permute-start.5) | collective-permute-done | bytes 90144 | tf_op jit(solution)/shard_map/ppermute | solution.py:301
  55.0 6.6 %collective-permute-done.6 = bf16[8,5632]{1,0:T(8,128)(2,1)S(1)} collective-permute-done((bf16[8,5632]{1,0:T(8,128)(2,1)S(1)}, bf16[8,5632]{1,0:T(8,128)(2,1)S(1)}, u32[]{:S(2)}, u32[]{:S(2)}) %collective-permute-start.6) | collective-permute-done | bytes 90144 | tf_op jit(solution)/shard_map/ppermute | solution.py:301
  62.6 3.0 %convolution_convert_fusion = bf16[64,512]{1,0:T(8,128)(2,1)S(1)} fusion(bf16[64,4096]{1,0:T(8,128)(2,1)S(1)} %slice_dynamic-update-slice_fusion, bf16[4096,512]{1,0:T(8,128)(2,1)} %bitcast.26), kind=kOutput, calls=%fused_computation.1 | convolution fusion | flops 268468224 | bytes 4784128 | tf_op jit(solution)/shard_map/dot_general | solution.py:320
  67.3 7.5 %all-to-all-start = ((bf16[32,64,512]{2,1,0:T(8,128)(2,1)}), bf16[32,64,512]{2,1,0:T(8,128)(2,1)S(1)}, u32[]{:S(2)}, u32[]{:S(2)}) async-start(bf16[32,64,512]{2,1,0:T(8,128)(2,1)} %broadcast_in_dim.95), calls=%async_computation | async-start | bytes 4194304 | tf_op jit(solution)/shard_map/all_to_all | solution.py:321
  89.0 9.5 %collective-permute-done.10.refs_4_ = bf16[2,256,256]{2,1,0:T(8,128)(2,1)S(1)} collective-permute-done((bf16[2,256,256]{2,1,0:T(8,128)(2,1)S(1)}, bf16[2,256,256]{2,1,0:T(8,128)(2,1)S(1)}, u32[]{:S(2)}, u32[]{:S(2)}) %collective-permute-start.10) | collective-permute-done | bytes 262176 | tf_op jit(solution)/shard_map/ppermute | solution.py:301
  98.4 3.9 %collective-permute-start.20 = (bf16[1,256,256]{2,1,0:T(8,128)(2,1)}, bf16[1,256,256]{2,1,0:T(8,128)(2,1)}, u32[]{:S(2)}, u32[]{:S(2)}) collective-permute-start(bf16[1,256,256]{2,1,0:T(8,128)(2,1)} %get-tuple-element.69), channel_id=1, source_target_pairs={{0,4},{1,5},{2,6},{3,7},{4,0},{5,1},{6,2},{7,3},{8,12},{9,13},{10,... | collective-permute-start | bytes 393224 | tf_op jit(solution)/shard_map/ppermute | solution.py:301
  104.0 7.6 %text_rows.1 = bf16[256,640]{1,0:T(8,128)(2,1)} custom-call(s32[1]{0:T(128)} %bitcast.lane_ref, bf16[8,128,768]{2,1,0:T(8,128)(2,1)} %bitcast.42, bf16[2048,512]{1,0:T(8,128)(2,1)} %bitcast.30, bf16[4096,512]{1,0:T(8,128)(2,1)} %bitcast.27, s32[1,128]{1,0:T(1,128)} %bitcast_add_fusion.slot_ref, s32[1,128]{1,0:T(1,128)} %sample_ref.1), custom_call_target="tpu_custom_call" | custom-call | flops 5500000256 | tf_op jit(solution)/shard_map/text_rows/pallas_call | solution.py:97
  111.6 8.5 %all-to-all-start.1 = ((bf16[32,8,640]{2,1,0:T(8,128)(2,1)}), bf16[32,8,640]{2,1,0:T(8,128)(2,1)S(1)}, u32[]{:S(2)}, u32[]{:S(2)}) async-start(bf16[32,8,640]{2,1,0:T(8,128)(2,1)} %bitcast.34), calls=%async_computation.1 | async-start | bytes 655360 | tf_op jit(solution)/shard_map/all_to_all | solution.py:352
  120.2 4.0 %collective-permute-start.22 = (bf16[1,256,256]{2,1,0:T(8,128)(2,1)S(1)}, bf16[1,256,256]{2,1,0:T(8,128)(2,1)S(1)}, u32[]{:S(2)}, u32[]{:S(2)}) collective-permute-start(bf16[1,256,256]{2,1,0:T(8,128)(2,1)S(1)} %copy-done.19), channel_id=1, source_target_pairs={{0,5},{1,6},{2,7},{3,0},{4,1},{5,2},{6,3},{7,4},{8,13},{9,14},{10,... | collective-permute-start | bytes 393224 | tf_op jit(solution)/shard_map/ppermute | solution.py:301
  124.2 5.7 %collective-permute-done.12.refs_6_ = bf16[2,256,256]{2,1,0:T(8,128)(2,1)} collective-permute-done((bf16[2,256,256]{2,1,0:T(8,128)(2,1)S(1)}, bf16[2,256,256]{2,1,0:T(8,128)(2,1)}, u32[]{:S(2)}, u32[]{:S(2)}) %collective-permute-start.12) | collective-permute-done | bytes 262176 | tf_op jit(solution)/shard_map/ppermute | solution.py:301
  134.0 4.9 %prepare.1 = (bf16[2,256,2816]{2,1,0:T(8,128)(2,1)}, bf16[2,2816,256]{2,1,0:T(8,128)(2,1)}) custom-call(s32[1]{0:T(128)} %bitcast.lane_ref, bf16[2048,128]{1,0:T(8,128)(2,1)} %select_convert_fusion.bar_ref, bf16[2,256,256]{2,1,0:T(8,128)(2,1)} %get-tuple-element.41.refs_0_, bf16[2,256,256]{2,1,0:T(8,128)(2,1)} %copy-done.9, bf16[2,256,256]{2,1,0:T(8,128)(2,1)} %copy-done.10, ...), custom_call_target="tpu_custom_call" | custom-call | flops 4400000000 | tf_op jit(solution)/shard_map/prepare/pallas_call | solution.py:148
  139.0 3.2 %collective-permute-start.17 = (bf16[1,256,256]{2,1,0:T(8,128)(2,1)S(1)}, bf16[1,256,256]{2,1,0:T(8,128)(2,1)S(1)}, u32[]{:S(2)}, u32[]{:S(2)}) collective-permute-start(bf16[1,256,256]{2,1,0:T(8,128)(2,1)S(1)} %copy-done.15), channel_id=1, source_target_pairs={{0,7},{1,0},{2,1},{3,2},{4,3},{5,4},{6,5},{7,6},{8,15},{9,8},{10,9... | collective-permute-start | bytes 393224 | tf_op jit(solution)/shard_map/ppermute | solution.py:301
  143.0 11.6 %attend.5 = (bf16[256,256]{1,0:T(8,128)(2,1)}, bf16[256,256]{1,0:T(8,128)(2,1)}, bf16[256,256]{1,0:T(8,128)(2,1)}) custom-call(s32[20]{0:T(128)} %pad_add_fusion.2.info_ref, bf16[2048,128]{1,0:T(8,128)(2,1)} %fusion.hot_ref, bf16[256,640]{1,0:T(8,128)(2,1)} %bitcast.31, bf16[2,256,2816]{2,1,0:T(8,128)(2,1)} %get-tuple-element.53.key_ref, ...), custom_call_target="tpu_custom_call" | custom-call | flops 11000000512 | tf_op jit(solution)/shard_map/attend/pallas_call | solution.py:229
  154.6 3.4 %collective-permute-start.24 = (bf16[256,256]{1,0:T(8,128)(2,1)}, bf16[256,256]{1,0:T(8,128)(2,1)S(1)}, u32[]{:S(2)}, u32[]{:S(2)}) collective-permute-start(bf16[256,256]{1,0:T(8,128)(2,1)} %get-tuple-element.73), channel_id=1, source_target_pairs={{0,4},{1,5},{2,6},{3,7},{4,0},{5,1},{6,2},{7,3},{8,12},{9,13},{10,... | collective-permute-start | bytes 393224 | tf_op jit(solution)/shard_map/ppermute | solution.py:301
  160.6 12.3 %attend.4 = (bf16[256,256]{1,0:T(8,128)(2,1)}, bf16[256,256]{1,0:T(8,128)(2,1)}, bf16[256,256]{1,0:T(8,128)(2,1)}, bf16[256,256]{1,0:T(8,128)(2,1)}) custom-call(s32[21]{0:T(128)} %pad_add_fusion.1.info_ref, bf16[2048,128]{1,0:T(8,128)(2,1)} %fusion.hot_ref, bf16[256,640]{1,0:T(8,128)(2,1)} %bitcast.32, bf16[2,256,2816]{2,1,0:T(8,128)(2,1)} %get-tuple-element.53.key_ref, ...), custom_call_target="tpu_custom_call" | custom-call | flops 14300000256 | tf_op jit(solution)/shard_map/attend/pallas_call | solution.py:229
  175.1 4.0 %collective-permute-start.19 = (bf16[256,256]{1,0:T(8,128)(2,1)}, bf16[256,256]{1,0:T(8,128)(2,1)S(1)}, u32[]{:S(2)}, u32[]{:S(2)}) collective-permute-start(bf16[256,256]{1,0:T(8,128)(2,1)} %get-tuple-element.68), channel_id=1, source_target_pairs={{0,6},{1,7},{2,0},{3,1},{4,2},{5,3},{6,4},{7,5},{8,14},{9,15},{10,... | collective-permute-start | bytes 393224 | tf_op jit(solution)/shard_map/ppermute | solution.py:301
  179.5 5.3 %attend.3.refs_0_ = bf16[256,256]{1,0:T(8,128)(2,1)} custom-call(s32[18]{0:T(128)} %pad_add_fusion.info_ref, bf16[2048,128]{1,0:T(8,128)(2,1)} %fusion.hot_ref, bf16[256,640]{1,0:T(8,128)(2,1)} %bitcast.33, bf16[2,256,2816]{2,1,0:T(8,128)(2,1)} %get-tuple-element.53.key_ref, bf16[2,2816,256]{2,1,0:T(8,128)(2,1)} %get-tuple-element.54.value_ref, ...), custom_call_target="tpu_custom_call" | custom-call | flops 4400000000 | tf_op jit(solution)/shard_map/attend/pallas_call | solution.py:229
  188.7 6.0 %project.1 = bf16[256,1536]{1,0:T(8,128)(2,1)} custom-call(s32[1]{0:T(128)} %bitcast.lane_ref, bf16[2048,1536]{1,0:T(8,128)(2,1)} %all-gather.4.cloned.1.call-done.weight_ref, f32[256,1536]{1,0:T(8,128)} %select_select_fusion.gate_ref, bf16[256,256]{1,0:T(8,128)(2,1)} %attend.3.refs_0_, bf16[256,256]{1,0:T(8,128)(2,1)} %copy-done.27, ...), custom_call_target="tpu_custom_call" | custom-call | flops 5500000256 | tf_op jit(solution)/shard_map/project/pallas_call | solution.py:261
  (166 shorter events, 41.5 us)
Async XLA Ops:
  6.5 97.5 %all-gather.6.cloned.1.call-start = ((), (), s32[]{:S(2)}) async-start(), calls=%async_computation.3 | async-start | bytes 1769472 | tf_op jit(solution)/shard_map/all_gather | solution.py:303
  8.1 19.9 %collective-permute-start.3 = (bf16[8,5632]{1,0:T(8,128)(2,1)S(1)}, bf16[8,5632]{1,0:T(8,128)(2,1)S(1)}, u32[]{:S(2)}, u32[]{:S(2)}) collective-permute-start(bf16[8,5632]{1,0:T(8,128)(2,1)S(1)} %pad_maximum_fusion.1), channel_id=1, source_target_pairs={{0,1},{1,2},{2,3},{3,4},{4,5},{5,6},{6,7},{7,0},{8,9},{9,10},{10,1... | collective-permute-start | bytes 270344 | tf_op jit(solution)/shard_map/ppermute | solution.py:301
  10.1 21.2 %collective-permute-start = (bf16[8,5632]{1,0:T(8,128)(2,1)S(1)}, bf16[8,5632]{1,0:T(8,128)(2,1)S(1)}, u32[]{:S(2)}, u32[]{:S(2)}) collective-permute-start(bf16[8,5632]{1,0:T(8,128)(2,1)S(1)} %pad_maximum_fusion.1), channel_id=1, source_target_pairs={{0,7},{1,0},{2,1},{3,2},{4,3},{5,4},{6,5},{7,6},{8,15},{9,8},{10,9... | collective-permute-start | bytes 270344 | tf_op jit(solution)/shard_map/ppermute | solution.py:301
  17.2 69.9 %collective-permute-start.13 = (bf16[2,256,256]{2,1,0:T(8,128)(2,1)}, bf16[2,256,256]{2,1,0:T(8,128)(2,1)S(1)}, u32[]{:S(2)}, u32[]{:S(2)}) collective-permute-start(bf16[2,256,256]{2,1,0:T(8,128)(2,1)} %get-tuple-element.48), channel_id=1, source_target_pairs={{0,7},{1,0},{2,1},{3,2},{4,3},{5,4},{6,5},{7,6},{8,15},{9,8},{10,9... | collective-permute-start | bytes 786440 | tf_op jit(solution)/shard_map/ppermute | solution.py:301
  19.2 69.3 %collective-permute-start.7 = (bf16[2,256,256]{2,1,0:T(8,128)(2,1)}, bf16[2,256,256]{2,1,0:T(8,128)(2,1)S(1)}, u32[]{:S(2)}, u32[]{:S(2)}) collective-permute-start(bf16[2,256,256]{2,1,0:T(8,128)(2,1)} %get-tuple-element.42), channel_id=1, source_target_pairs={{0,1},{1,2},{2,3},{3,4},{4,5},{5,6},{6,7},{7,0},{8,9},{9,10},{10,1... | collective-permute-start | bytes 786440 | tf_op jit(solution)/shard_map/ppermute | solution.py:301
  19.3 69.7 %collective-permute-start.8 = (bf16[2,256,256]{2,1,0:T(8,128)(2,1)}, bf16[2,256,256]{2,1,0:T(8,128)(2,1)S(1)}, u32[]{:S(2)}, u32[]{:S(2)}) collective-permute-start(bf16[2,256,256]{2,1,0:T(8,128)(2,1)} %get-tuple-element.43), channel_id=1, source_target_pairs={{0,2},{1,3},{2,4},{3,5},{4,6},{5,7},{6,0},{7,1},{8,10},{9,11},{10,... | collective-permute-start | bytes 786440 | tf_op jit(solution)/shard_map/ppermute | solution.py:301
  20.4 167.7 %all-gather.4.cloned.1.call-start = ((), (), s32[]{:S(2)}) async-start(), calls=%async_computation.2 | async-start | bytes 6488064 | tf_op jit(solution)/shard_map/all_gather | solution.py:323
  28.0 18.9 %collective-permute-start.4 = (bf16[8,5632]{1,0:T(8,128)(2,1)S(1)}, bf16[8,5632]{1,0:T(8,128)(2,1)S(1)}, u32[]{:S(2)}, u32[]{:S(2)}) collective-permute-start(bf16[8,5632]{1,0:T(8,128)(2,1)S(1)} %collective-permute-done.3), channel_id=1, source_target_pairs={{0,1},{1,2},{2,3},{3,4},{4,5},{5,6},{6,7},{7,0},{8,9},{9,10},{10,1... | collective-permute-start | bytes 270344 | tf_op jit(solution)/shard_map/ppermute | solution.py:301
  67.3 35.1 %all-to-all-start = ((bf16[32,64,512]{2,1,0:T(8,128)(2,1)}), bf16[32,64,512]{2,1,0:T(8,128)(2,1)S(1)}, u32[]{:S(2)}, u32[]{:S(2)}) async-start(bf16[32,64,512]{2,1,0:T(8,128)(2,1)} %broadcast_in_dim.95), calls=%async_computation | async-start | bytes 4194304 | tf_op jit(solution)/shard_map/all_to_all | solution.py:321
  81.7 16.8 %collective-permute-start.10 = (bf16[2,256,256]{2,1,0:T(8,128)(2,1)S(1)}, bf16[2,256,256]{2,1,0:T(8,128)(2,1)S(1)}, u32[]{:S(2)}, u32[]{:S(2)}) collective-permute-start(bf16[2,256,256]{2,1,0:T(8,128)(2,1)S(1)} %copy-done.13), channel_id=1, source_target_pairs={{0,4},{1,5},{2,6},{3,7},{4,0},{5,1},{6,2},{7,3},{8,12},{9,13},{10,... | collective-permute-start | bytes 786440 | tf_op jit(solution)/shard_map/ppermute | solution.py:301
  84.8 35.4 %collective-permute-start.11 = (bf16[2,256,256]{2,1,0:T(8,128)(2,1)}, bf16[2,256,256]{2,1,0:T(8,128)(2,1)}, u32[]{:S(2)}, u32[]{:S(2)}) collective-permute-start(bf16[2,256,256]{2,1,0:T(8,128)(2,1)} %get-tuple-element.51), channel_id=1, source_target_pairs={{0,5},{1,6},{2,7},{3,0},{4,1},{5,2},{6,3},{7,4},{8,13},{9,14},{10,... | collective-permute-start | bytes 786440 | tf_op jit(solution)/shard_map/ppermute | solution.py:301
  87.1 42.8 %collective-permute-start.12 = (bf16[2,256,256]{2,1,0:T(8,128)(2,1)S(1)}, bf16[2,256,256]{2,1,0:T(8,128)(2,1)}, u32[]{:S(2)}, u32[]{:S(2)}) collective-permute-start(bf16[2,256,256]{2,1,0:T(8,128)(2,1)S(1)} %copy-done.12), channel_id=1, source_target_pairs={{0,6},{1,7},{2,0},{3,1},{4,2},{5,3},{6,4},{7,5},{8,14},{9,15},{10,... | collective-permute-start | bytes 786440 | tf_op jit(solution)/shard_map/ppermute | solution.py:301
  88.4 43.5 %collective-permute-start.9 = (bf16[2,256,256]{2,1,0:T(8,128)(2,1)S(1)}, bf16[2,256,256]{2,1,0:T(8,128)(2,1)}, u32[]{:S(2)}, u32[]{:S(2)}) collective-permute-start(bf16[2,256,256]{2,1,0:T(8,128)(2,1)S(1)} %copy-done.11), channel_id=1, source_target_pairs={{0,3},{1,4},{2,5},{3,6},{4,7},{5,0},{6,1},{7,2},{8,11},{9,12},{10,... | collective-permute-start | bytes 786440 | tf_op jit(solution)/shard_map/ppermute | solution.py:301
  98.4 40.5 %collective-permute-start.20 = (bf16[1,256,256]{2,1,0:T(8,128)(2,1)}, bf16[1,256,256]{2,1,0:T(8,128)(2,1)}, u32[]{:S(2)}, u32[]{:S(2)}) collective-permute-start(bf16[1,256,256]{2,1,0:T(8,128)(2,1)} %get-tuple-element.69), channel_id=1, source_target_pairs={{0,4},{1,5},{2,6},{3,7},{4,0},{5,1},{6,2},{7,3},{8,12},{9,13},{10,... | collective-permute-start | bytes 393224 | tf_op jit(solution)/shard_map/ppermute | solution.py:301
  102.4 36.6 %collective-permute-start.21 = (bf16[1,256,256]{2,1,0:T(8,128)(2,1)}, bf16[1,256,256]{2,1,0:T(8,128)(2,1)}, u32[]{:S(2)}, u32[]{:S(2)}) collective-permute-start(bf16[1,256,256]{2,1,0:T(8,128)(2,1)} %get-tuple-element.70), channel_id=1, source_target_pairs={{0,3},{1,4},{2,5},{3,6},{4,7},{5,0},{6,1},{7,2},{8,11},{9,12},{10,... | collective-permute-start | bytes 393224 | tf_op jit(solution)/shard_map/ppermute | solution.py:301
  111.6 30.6 %all-to-all-start.1 = ((bf16[32,8,640]{2,1,0:T(8,128)(2,1)}), bf16[32,8,640]{2,1,0:T(8,128)(2,1)S(1)}, u32[]{:S(2)}, u32[]{:S(2)}) async-start(bf16[32,8,640]{2,1,0:T(8,128)(2,1)} %bitcast.34), calls=%async_computation.1 | async-start | bytes 655360 | tf_op jit(solution)/shard_map/all_to_all | solution.py:352
  120.2 22.1 %collective-permute-start.22 = (bf16[1,256,256]{2,1,0:T(8,128)(2,1)S(1)}, bf16[1,256,256]{2,1,0:T(8,128)(2,1)S(1)}, u32[]{:S(2)}, u32[]{:S(2)}) collective-permute-start(bf16[1,256,256]{2,1,0:T(8,128)(2,1)S(1)} %copy-done.19), channel_id=1, source_target_pairs={{0,5},{1,6},{2,7},{3,0},{4,1},{5,2},{6,3},{7,4},{8,13},{9,14},{10,... | collective-permute-start | bytes 393224 | tf_op jit(solution)/shard_map/ppermute | solution.py:301
  129.9 24.7 %collective-permute-start.14 = (bf16[1,256,256]{2,1,0:T(8,128)(2,1)S(1)}, bf16[1,256,256]{2,1,0:T(8,128)(2,1)S(1)}, u32[]{:S(2)}, u32[]{:S(2)}) collective-permute-start(bf16[1,256,256]{2,1,0:T(8,128)(2,1)S(1)} %copy-done.18), channel_id=1, source_target_pairs={{0,2},{1,3},{2,4},{3,5},{4,6},{5,7},{6,0},{7,1},{8,10},{9,11},{10,... | collective-permute-start | bytes 393224 | tf_op jit(solution)/shard_map/ppermute | solution.py:301
  131.9 26.0 %collective-permute-start.15 = (bf16[1,256,256]{2,1,0:T(8,128)(2,1)S(1)}, bf16[1,256,256]{2,1,0:T(8,128)(2,1)S(1)}, u32[]{:S(2)}, u32[]{:S(2)}) collective-permute-start(bf16[1,256,256]{2,1,0:T(8,128)(2,1)S(1)} %copy-done.17), channel_id=1, source_target_pairs={{0,6},{1,7},{2,0},{3,1},{4,2},{5,3},{6,4},{7,5},{8,14},{9,15},{10,... | collective-permute-start | bytes 393224 | tf_op jit(solution)/shard_map/ppermute | solution.py:301
  138.9 20.4 %collective-permute-start.16 = (bf16[1,256,256]{2,1,0:T(8,128)(2,1)S(1)}, bf16[1,256,256]{2,1,0:T(8,128)(2,1)S(1)}, u32[]{:S(2)}, u32[]{:S(2)}) collective-permute-start(bf16[1,256,256]{2,1,0:T(8,128)(2,1)S(1)} %copy-done.16), channel_id=1, source_target_pairs={{0,1},{1,2},{2,3},{3,4},{4,5},{5,6},{6,7},{7,0},{8,9},{9,10},{10,1... | collective-permute-start | bytes 393224 | tf_op jit(solution)/shard_map/ppermute | solution.py:301
  139.0 20.3 %collective-permute-start.17 = (bf16[1,256,256]{2,1,0:T(8,128)(2,1)S(1)}, bf16[1,256,256]{2,1,0:T(8,128)(2,1)S(1)}, u32[]{:S(2)}, u32[]{:S(2)}) collective-permute-start(bf16[1,256,256]{2,1,0:T(8,128)(2,1)S(1)} %copy-done.15), channel_id=1, source_target_pairs={{0,7},{1,0},{2,1},{3,2},{4,3},{5,4},{6,5},{7,6},{8,15},{9,8},{10,9... | collective-permute-start | bytes 393224 | tf_op jit(solution)/shard_map/ppermute | solution.py:301
  154.6 24.5 %collective-permute-start.23 = (bf16[256,256]{1,0:T(8,128)(2,1)}, bf16[256,256]{1,0:T(8,128)(2,1)S(1)}, u32[]{:S(2)}, u32[]{:S(2)}) collective-permute-start(bf16[256,256]{1,0:T(8,128)(2,1)} %get-tuple-element.72), channel_id=1, source_target_pairs={{0,5},{1,6},{2,7},{3,0},{4,1},{5,2},{6,3},{7,4},{8,13},{9,14},{10,... | collective-permute-start | bytes 393224 | tf_op jit(solution)/shard_map/ppermute | solution.py:301
  154.6 24.5 %collective-permute-start.24 = (bf16[256,256]{1,0:T(8,128)(2,1)}, bf16[256,256]{1,0:T(8,128)(2,1)S(1)}, u32[]{:S(2)}, u32[]{:S(2)}) collective-permute-start(bf16[256,256]{1,0:T(8,128)(2,1)} %get-tuple-element.73), channel_id=1, source_target_pairs={{0,4},{1,5},{2,6},{3,7},{4,0},{5,1},{6,2},{7,3},{8,12},{9,13},{10,... | collective-permute-start | bytes 393224 | tf_op jit(solution)/shard_map/ppermute | solution.py:301
  158.0 26.9 %collective-permute-start.25 = (bf16[256,256]{1,0:T(8,128)(2,1)}, bf16[256,256]{1,0:T(8,128)(2,1)S(1)}, u32[]{:S(2)}, u32[]{:S(2)}) collective-permute-start(bf16[256,256]{1,0:T(8,128)(2,1)} %get-tuple-element.74), channel_id=1, source_target_pairs={{0,3},{1,4},{2,5},{3,6},{4,7},{5,0},{6,1},{7,2},{8,11},{9,12},{10,... | collective-permute-start | bytes 393224 | tf_op jit(solution)/shard_map/ppermute | solution.py:301
  (41 other events, 341.3 us)
Sparse Core Ops, SparseCore 0:
  20.5 43.5 all-gather.5
  66.6 65.6 all-gather.3
